TPU v7x, 32 devices: a whole 2x2x4 slice. The times are simulated.
32 devices in a mesh: seq: 16 (over z, y, x), tp: 2 (over core).
Axes of the slice: x: 2, y: 2, z: 4, core: 2. Of those that a mesh axis runs over, the one named last changes fastest.
Arguments:
- hidden_in: bfloat16 [4096, 2048], P('seq')
- token_order: int32 [4096], P('seq'), may hold values from 0 to 4095, as said below
- span_lengths: int32 [4], replicated, may hold values from 1 to 2048, 4096 in all
- placement: int32 [32], replicated, may hold values from 0 to 31, as said below
- norm_in: float32 [2048], replicated, may hold values from 0.1 to 1.9
- q_weight: bfloat16 [2048, 2048], P(None, 'tp')
- k_weight: bfloat16 [2048, 1024], P(None, 'tp')
- v_weight: bfloat16 [2048, 1024], P(None, 'tp'), may hold values from -0.125 to 0.125
- q_gain: float32 [128], replicated
- k_gain: float32 [128], replicated
- o_weight: bfloat16 [2048, 2048], P('tp'), may hold values from -0.125 to 0.125
- norm_mid: float32 [2048], replicated, may hold values from 0.1 to 1.9
- gate_weight: bfloat16 [2048, 3072], P(None, 'tp'), may hold values from -0.125 to 0.125
- up_weight: bfloat16 [2048, 3072], P(None, 'tp'), may hold values from -0.125 to 0.125
- down_weight: bfloat16 [3072, 2048], P('tp'), may hold values from -0.109375 to 0.109375
Outputs:
- hidden_out: bfloat16 [4096, 2048], P('seq', 'tp')
- kv_cache: bfloat16 [32, 128, 2048], P('seq', None, 'tp')
Inputs may be any that keep to these rules, and one draw needn't show every extreme that they name: `token_order`: a permutation of all tokens; for each block b of 128 consecutive tokens and each seq index d, rows d * 256 + placement[b] * 8 + j, j < 8, hold tokens of block b. `placement`: a permutation of the blocks. `span_lengths`: sum to 4096.
All inputs are finite; a program needn't handle non-finite values.
Results may differ from a plain program's by a relative error of at most 0.022.
The roundings to bfloat16 on the way count: a program that leaves them out, or rounds other values in their place, can miss the bound.
Values may be sent and summed in bfloat16 or wider, within the bound.
A program may use at most 128 MiB of HBM per device.

v0:
```python
import jax
import jax.numpy as jnp
from jax import lax
from jax.sharding import PartitionSpec as P

HD = 128
BLK = 128


EPS = 1e-06
THETA = 1000000.0


def rms(values, gain):
    return values * lax.rsqrt(jnp.mean(values * values, axis=-1, keepdims=True) + EPS) * gain


def rotary(values, pos):
    half = values.shape[-1] // 2
    freq = THETA ** (-jnp.arange(half, dtype=jnp.float32) * 2.0 / values.shape[-1])
    angle = pos.astype(jnp.float32)[:, None] * freq[None, :]
    cosine = jnp.cos(angle)[:, None, :]
    sine = jnp.sin(angle)[:, None, :]
    first = values[..., :half]
    second = values[..., half:]
    return jnp.concatenate(
        [first * cosine - second * sine, second * cosine + first * sine], axis=-1
    )


def request_start(order, lengths):
    ends = jnp.cumsum(lengths)
    begins = ends - lengths
    return jnp.max(jnp.where(begins[None, :] <= order[:, None], begins[None, :], 0), axis=1)


def relay_cache(stacked, token_order, rows, seq_count):
    arrived, anchor = (
        lax.all_to_all(stacked, "seq", split_axis=0, concat_axis=0, tiled=True),
        lax.all_to_all(token_order, "seq", split_axis=0, concat_axis=0, tiled=True),
    )
    group_rows = rows // seq_count
    share = BLK // seq_count
    local_slot = jnp.arange(rows, dtype=jnp.int32) % group_rows // share
    target = local_slot * BLK + anchor % BLK
    cache = jnp.zeros(stacked.shape, jnp.bfloat16).at[target].set(arrived)
    return cache.reshape(rows // BLK, BLK, stacked.shape[1])


def body(
    hidden_in,
    token_order,
    span_lengths,
    placement,
    norm_in,
    q_weight,
    k_weight,
    v_weight,
    q_gain,
    k_gain,
    o_weight,
    norm_mid,
    gate_weight,
    up_weight,
    down_weight,
):
    rows, width = hidden_in.shape
    seq_count = lax.axis_size("seq")
    tp_count = lax.axis_size("tp")
    part = width // tp_count
    kv_heads = k_weight.shape[1] // HD
    q_heads = q_weight.shape[1] // HD
    group = q_heads // kv_heads
    xfull = hidden_in.astype(jnp.float32)
    normed = rms(xfull, norm_in).astype(jnp.bfloat16)
    begin = request_start(token_order, span_lengths)
    pos = token_order - begin
    query = jnp.dot(normed, q_weight, preferred_element_type=jnp.float32).reshape(rows, q_heads, HD)
    keys = jnp.dot(normed, k_weight, preferred_element_type=jnp.float32).reshape(rows, kv_heads, HD)
    values = (
        jnp.dot(normed, v_weight, preferred_element_type=jnp.float32)
        .reshape(rows, kv_heads, HD)
        .astype(jnp.bfloat16)
    )
    qnorm = rotary(rms(query, q_gain), pos).astype(jnp.bfloat16).reshape(rows, kv_heads, group, HD)
    knorm = rotary(rms(keys, k_gain), pos).astype(jnp.bfloat16)
    stacked = jnp.stack([knorm, values], axis=2).reshape(rows, kv_heads * 2 * HD)
    scale = 1.0 / HD**0.5
    start_best = jnp.full((rows, kv_heads, group), -1e30, jnp.float32)
    best = start_best
    piece_keys = lax.all_gather(knorm, "seq", axis=0, tiled=True)
    piece_values = lax.all_gather(values, "seq", axis=0, tiled=True)
    piece_order = lax.all_gather(token_order, "seq", axis=0, tiled=True)
    score = (
        jnp.einsum("qkge,nke->qkgn", qnorm, piece_keys, preferred_element_type=jnp.float32) * scale
    )
    mask = (piece_order[None, :] >= begin[:, None]) & (piece_order[None, :] <= token_order[:, None])
    mask = mask[:, None, None, :]
    score = jnp.where(mask, score, -1e30)
    new_best = jnp.maximum(best, jnp.max(score, axis=-1))
    weights = jnp.where(mask, jnp.exp(score - new_best[..., None]), 0.0)
    total = jnp.sum(weights, axis=-1)
    accum = jnp.einsum(
        "qkgn,nke->qkge",
        weights.astype(jnp.bfloat16),
        piece_values,
        preferred_element_type=jnp.float32,
    )
    best, total, accum = (new_best, total, accum)
    attn = (accum / total[..., None]).astype(jnp.bfloat16).reshape(rows, q_heads * HD)
    terms = jnp.dot(attn, o_weight, preferred_element_type=jnp.float32)
    column = lax.axis_index("tp") * part
    own_input = lax.dynamic_slice_in_dim(xfull, column, part, 1)
    mid = (
        own_input
        + lax.psum_scatter(
            terms.astype(jnp.bfloat16), "tp", scatter_dimension=1, tiled=True
        ).astype(jnp.float32)
    ).astype(jnp.bfloat16)
    mid_full = lax.all_gather(mid, "tp", axis=1, tiled=True)
    normed_mid = rms(mid_full.astype(jnp.float32), norm_mid).astype(jnp.bfloat16)
    gate = jnp.dot(normed_mid, gate_weight, preferred_element_type=jnp.float32)
    upper = jnp.dot(normed_mid, up_weight, preferred_element_type=jnp.float32)
    act = (jax.nn.silu(gate) * upper).astype(jnp.bfloat16)
    feed = lax.psum_scatter(
        jnp.dot(act, down_weight, preferred_element_type=jnp.float32).astype(jnp.bfloat16),
        "tp",
        scatter_dimension=1,
        tiled=True,
    ).astype(jnp.float32)
    out = (mid.astype(jnp.float32) + feed).astype(jnp.bfloat16)
    blocks_dev = rows // BLK
    share = BLK // seq_count
    slots = placement.reshape(seq_count, blocks_dev)
    send_rows = (
        slots[:, :, None] * share + jnp.arange(share, dtype=jnp.int32)[None, None, :]
    ).reshape(rows)
    arrived, anchor = (
        lax.all_to_all(out[send_rows], "seq", split_axis=0, concat_axis=0, tiled=True),
        lax.all_to_all(token_order[send_rows], "seq", split_axis=0, concat_axis=0, tiled=True),
    )
    local_row = anchor - lax.axis_index("seq") * rows
    hidden_out = jnp.zeros_like(out).at[local_row].set(arrived)
    kv_cache = relay_cache(stacked, token_order, rows, seq_count)
    return (hidden_out, kv_cache)


def solution(mesh):
    in_specs = (
        P("seq", None),
        P("seq"),
        P(),
        P(),
        P(),
        P(None, "tp"),
        P(None, "tp"),
        P(None, "tp"),
        P(),
        P(),
        P("tp", None),
        P(),
        P(None, "tp"),
        P(None, "tp"),
        P("tp", None),
    )
    out_specs = (P("seq", "tp"), P("seq", None, "tp"))
    return jax.shard_map(body, mesh=mesh, in_specs=in_specs, out_specs=out_specs, check_vma=False)
```

profile of v0, /device:TPU:14, one launch (start us, length us, event | category | flops | bytes accessed | tf_op | source)
XLA Modules:
  0.0 310.1 jit_solution(17099454060054883808)
XLA Ops:
  7.3 1.6 multiply_reduce_fusion
  9.1 2.9 fusion.47
  16.9 2.4 convolution_convert_fusion.2
  20.3 3.5 %convolution_bitcast_fusion = f32[32,8,8,128]{3,1,2,0:T(8,128)S(1)} fusion(bf16[2048,1024]{1,0:T(8,128)(2,1)} %param.20, f32[2048]{0:T(1024)S(1)} %copy-done.13, f32[256]{0:T(256)S(1)} %add_rsqrt_fusion.3, bf16[256,2048]{1,0:T(8,128)(2,1)S(1)} %copy-done.4), kind=kOutput, calls=%fused_computation.27 | convolution fusion | flops 1075838976 | bytes 6300672 | tf_op jit(solution)/shard_map/dot_general | solution.py:78
  26.5 1.4 subtract_convert_fusion
  28.1 28.6 %all-gather = s32[16,1,256]{2,1,0:T(1,128)S(1)} all-gather(s32[1,1,256]{2,1,0:T(1,128)S(1)} %bitcast.79), channel_id=1, replica_groups=mesh['seq'=16,'tp'=2] {'seq'}, dimensions={0}, use_global_device_ids=true | all-gather | bytes 17408 | tf_op jit(solution)/shard_map/all_gather | solution.py:93
  56.7 1.9 compare_and_fusion
  58.6 34.7 %all-gather.7.cloned.1.call-done = bf16[4096,4,128]{2,0,1:T(8,128)(2,1)} async-done(((bf16[256,4,128]{2,0,1:T(8,128)(2,1)}), bf16[4096,4,128]{2,0,1:T(8,128)(2,1)}) %all-gather.7.cloned.1.call-update) | async-done | bytes 4194320 | tf_op jit(solution)/shard_map/all_gather | solution.py:91
  93.2 16.0 %fusion = (f32[256,4,2]{0,2,1:T(2,128)S(1)}, f32[4,4096,256,2]{2,1,3,0:T(8,128)}) fusion(pred[256,4096]{0,1:T(8,128)(4,1)S(1)} %compare_and_fusion, bf16[256,4,2,64]{3,0,2,1:T(8,128)(2,1)S(1)} %bitcast.87, bf16[256,4,2,64]{3,0,2,1:T(8,128)(2,1)S(1)} %bitcast.86, bf16[4096,4,128]{2,0,1:T(8,128)(2,1)} %all-gather.7.cloned.1.call-done), kind=kOutput, calls=%fused_computation.6 | convolution fusion | flops 2173696000 | bytes 39329792 | tf_op jit(solution)/shard_map/qkge,nke->qkgn/dot_general | solution.py:95
  109.2 14.9 %fusion.1 = f32[256,4,2]{0,2,1:T(2,128)S(1)} fusion(f32[4,4096,256,2]{2,1,3,0:T(8,128)} %get-tuple-element.9, f32[256,4,2]{0,2,1:T(2,128)S(1)} %broadcast_maximum_fusion, pred[256,4096]{0,1:T(8,128)(4,1)S(1)} %compare_and_fusion), kind=kLoop, calls=%fused_computation.7 | loop fusion | flops 41940992 | bytes 34619392 | tf_op jit(solution)/shard_map/reduce_sum | solution.py:102
  124.2 56.3 %all-gather.5.cloned.1.call-done = bf16[4096,4,128]{0,2,1:T(8,128)(2,1)} async-done(((bf16[256,4,128]{0,2,1:T(8,128)(2,1)}), bf16[4096,4,128]{0,2,1:T(8,128)(2,1)}) %all-gather.5.cloned.1.call-update) | async-done | bytes 4194320 | tf_op jit(solution)/shard_map/all_gather | solution.py:92
  180.5 15.8 %fusion.23 = bf16[256,4,2,128]{0,3,2,1:T(8,128)(2,1)S(1)} fusion(f32[4,4096,256,2]{2,1,3,0:T(8,128)} %get-tuple-element.9, f32[256,4,2]{0,2,1:T(2,128)S(1)} %broadcast_maximum_fusion, pred[256,4096]{0,1:T(8,128)(4,1)S(1)} %compare_and_fusion, bf16[4096,4,128]{0,2,1:T(8,128)(2,1)} %all-gather.5.cloned.1.call-done, f32[256,4,2]{0,2,1:T(2,128)S(1)} %fusion.1), kind=kOutput, calls=%fused_computation.29 | convolution fusion | flops 2189950976 | bytes 39337984 | tf_op jit(solution)/shard_map/qkgn,nke->qkge/dot_general | solution.py:103
  196.3 4.4 %convolution_convert_fusion.1 = bf16[256,2048]{1,0:T(8,128)(2,1)} fusion(bf16[256,1024]{0,1:T(8,128)(2,1)S(1)} %bitcast.93, bf16[1024,2048]{1,0:T(8,128)(2,1)} %param.25), kind=kOutput, calls=%fused_computation.20 | convolution fusion | flops 1074266112 | bytes 5767168 | tf_op jit(solution)/shard_map/dot_general | solution.py:111
  201.0 9.6 %reduce-scatter.3.cloned.1.call-done = bf16[256,1024]{1,0:T(8,128)(2,1)} async-done(((bf16[256,2048]{1,0:T(8,128)(2,1)}), bf16[256,1024]{1,0:T(8,128)(2,1)}) %reduce-scatter.3.cloned.1.call-update) | async-done | bytes 524304 | tf_op jit(solution)/shard_map/reduce_scatter | solution.py:116
  210.6 2.0 add_convert_fusion.1
  212.9 10.1 %all-gather.9.cloned.1.call-done = bf16[256,2048]{1,0:T(8,128)(2,1)} async-done(((bf16[256,1024]{1,0:T(8,128)(2,1)}), bf16[256,2048]{1,0:T(8,128)(2,1)}) %all-gather.9.cloned.1.call-update) | async-done | bytes 1048592 | tf_op jit(solution)/shard_map/all_gather | solution.py:120
  223.0 1.5 fusion.10
  224.5 6.2 %fusion.34 = f32[256,1536]{1,0:T(8,128)} fusion(bf16[2048,1536]{1,0:T(8,128)(2,1)} %param.27, bf16[256,2048]{1,0:T(8,128)(2,1)} %all-gather.9.cloned.1.call-done, f32[2048]{0:T(1024)S(1)} %copy-done.14, f32[256]{0:T(256)S(1)} %add_rsqrt_fusion.2), kind=kOutput, calls=%fused_computation.46 | convolution fusion | flops 1612709888 | bytes 8922112 | tf_op jit(solution)/shard_map/dot_general | solution.py:122
  230.7 9.6 %convolution_convert_fusion = bf16[256,2048]{1,0:T(8,128)(2,1)} fusion(bf16[1536,2048]{1,0:T(8,128)(2,1)} %param.29, bf16[2048,1536]{1,0:T(8,128)(2,1)} %param.28, f32[256,1536]{1,0:T(8,128)} %fusion.34, bf16[256,2048]{1,0:T(8,128)(2,1)S(1)} %copy-done.8, f32[2048]{0:T(1024)S(1)} %copy-done.14, f32[256]{0:T(256)S(1)} %add_rsqrt_fusion.2), kind=kOutput, calls=%fused_computation.19 | convolution fusion | flops 3226206208 | bytes 16262144 | tf_op jit(solution)/shard_map/dot_general | solution.py:126
  240.7 1.9 gather_fusion
  243.3 7.0 %all-to-all-start = ((s32[16,16,1]{1,2,0:T(1,128)}), s32[16,16,1]{1,2,0:T(1,128)S(1)}, u32[]{:S(2)}, u32[]{:S(2)}) async-start(s32[16,16,1]{1,2,0:T(1,128)} %all_to_all.30), calls=%async_computation | async-start | bytes 16384 | tf_op jit(solution)/shard_map/all_to_all | solution.py:140
  251.1 3.3 %all-to-all-done = s32[16,16,1]{1,2,0:T(1,128)S(1)} async-done(((s32[16,16,1]{1,2,0:T(1,128)}), s32[16,16,1]{1,2,0:T(1,128)S(1)}, u32[]{:S(2)}, u32[]{:S(2)}) %all-to-all-start) | async-done | bytes 1056 | tf_op jit(solution)/shard_map/all_to_all | solution.py:140
  254.3 6.5 %all-to-all-start.2 = ((s32[16,16,1]{1,2,0:T(1,128)}), s32[16,16,1]{1,2,0:T(1,128)S(1)}, u32[]{:S(2)}, u32[]{:S(2)}) async-start(s32[16,16,1]{1,2,0:T(1,128)} %all_to_all.35), calls=%async_computation.4 | async-start | bytes 16384 | tf_op jit(solution)/shard_map/all_to_all | solution.py:40
  262.8 2.3 all-to-all-done.2
  265.0 7.2 %all-to-all-start.3 = ((bf16[16,16,1024]{2,1,0:T(8,128)(2,1)}), bf16[16,16,1024]{2,1,0:T(8,128)(2,1)}, u32[]{:S(2)}, u32[]{:S(2)}) async-start(bf16[16,16,1024]{2,1,0:T(8,128)(2,1)} %all_to_all.38), calls=%async_computation.5 | async-start | bytes 1048576 | tf_op jit(solution)/shard_map/all_to_all | solution.py:39
  272.3 1.4 add_convert_fusion
  273.7 2.0 gather_fusion.1
  275.7 8.0 %all-to-all-done.3 = bf16[16,16,1024]{2,1,0:T(8,128)(2,1)} async-done(((bf16[16,16,1024]{2,1,0:T(8,128)(2,1)}), bf16[16,16,1024]{2,1,0:T(8,128)(2,1)}, u32[]{:S(2)}, u32[]{:S(2)}) %all-to-all-start.3) | async-done | bytes 524320 | tf_op jit(solution)/shard_map/all_to_all | solution.py:39
  283.7 5.9 %all-to-all-start.1 = ((bf16[16,16,1024]{2,1,0:T(8,128)(2,1)}), bf16[16,16,1024]{2,1,0:T(8,128)(2,1)S(1)}, u32[]{:S(2)}, u32[]{:S(2)}) async-start(bf16[16,16,1024]{2,1,0:T(8,128)(2,1)} %bitcast.16), calls=%async_computation.3 | async-start | bytes 1048576 | tf_op jit(solution)/shard_map/all_to_all | solution.py:139
  291.0 3.0 scatter_custom_fusion.1
  294.0 7.2 %all-to-all-done.1 = bf16[16,16,1024]{2,1,0:T(8,128)(2,1)S(1)} async-done(((bf16[16,16,1024]{2,1,0:T(8,128)(2,1)}), bf16[16,16,1024]{2,1,0:T(8,128)(2,1)S(1)}, u32[]{:S(2)}, u32[]{:S(2)}) %all-to-all-start.1) | async-done | bytes 524320 | tf_op jit(solution)/shard_map/all_to_all | solution.py:139
  301.2 2.4 scatter_custom_fusion
  (91 shorter events, 14.5 us)
Async XLA Ops:
  7.2 1.9 copy-start
  7.2 6.4 %copy-start.15 = (s32[4]{0:T(128)S(1)}, s32[4]{0:T(128)}, u32[]{:S(2)}) copy-start(s32[4]{0:T(128)} %param.17) | copy-start | bytes 52
  7.2 6.6 %copy-start.2 = (s32[256]{0:T(256)S(1)}, s32[256]{0:T(256)}, u32[]{:S(2)}) copy-start(s32[256]{0:T(256)} %param.16) | copy-start | bytes 3076
  7.2 6.7 %copy-start.11 = (f32[128]{0:T(128)S(1)}, f32[128]{0:T(128)}, u32[]{:S(2)}) copy-start(f32[128]{0:T(128)} %param.24) | copy-start | bytes 1540
  7.2 86.0 %all-gather.7.cloned.1.call-start = ((), (), s32[]{:S(2)}) async-start(), calls=%async_computation.7 | async-start | bytes 4456448 | tf_op jit(solution)/shard_map/all_gather | solution.py:91
  9.1 7.8 %copy-start.4 = (bf16[256,2048]{1,0:T(8,128)(2,1)S(1)}, bf16[256,2048]{1,0:T(8,128)(2,1)}, u32[]{:S(2)}) copy-start(bf16[256,2048]{1,0:T(8,128)(2,1)} %param.15) | copy-start | bytes 3145732
  12.0 5.0 %copy-start.13 = (f32[2048]{0:T(1024)S(1)}, f32[2048]{0:T(1024)}, u32[]{:S(2)}) copy-start(f32[2048]{0:T(1024)} %param.19) | copy-start | bytes 24580
  15.7 4.5 %copy-start.7 = (f32[256,64]{1,0:T(8,128)}, f32[256,64]{1,0:T(8,128)S(1)}, u32[]{:S(2)}) copy-start(f32[256,64]{1,0:T(8,128)S(1)} %get-tuple-element.7) | copy-start | bytes 196612
  16.0 4.3 %copy-start.5 = (bf16[256,4,64]{2,0,1:T(8,128)(2,1)}, bf16[256,4,64]{2,0,1:T(8,128)(2,1)S(1)}, u32[]{:S(2)}) copy-start(bf16[256,4,64]{2,0,1:T(8,128)(2,1)S(1)} %get-tuple-element.5) | copy-start | bytes 393220
  16.9 163.6 %all-gather.5.cloned.1.call-start = ((), (), s32[]{:S(2)}) async-start(), calls=%async_computation.6 | async-start | bytes 4456448 | tf_op jit(solution)/shard_map/all_gather | solution.py:92
  19.3 1.0 copy-start.9
  20.2 5.0 %copy-start.12 = (f32[128]{0:T(128)S(1)}, f32[128]{0:T(128)}, u32[]{:S(2)}) copy-start(f32[128]{0:T(128)} %param.23) | copy-start | bytes 1540
  20.2 190.4 %reduce-scatter.3.cloned.1.call-start = ((), (), s32[]{:S(2)}) async-start(), calls=%async_computation.8 | async-start | bytes 1572864 | tf_op jit(solution)/shard_map/reduce_scatter | solution.py:116
  200.7 23.8 %copy-start.14 = (f32[2048]{0:T(1024)S(1)}, f32[2048]{0:T(1024)}, u32[]{:S(2)}) copy-start(f32[2048]{0:T(1024)} %param.26) | copy-start | bytes 24580
  200.7 22.2 %all-gather.9.cloned.1.call-start = ((), (), s32[]{:S(2)}) async-start(), calls=%async_computation.9 | async-start | bytes 1572864 | tf_op jit(solution)/shard_map/all_gather | solution.py:120
  212.6 59.7 %reduce-scatter.5.cloned.1.call-start = ((), (), s32[]{:S(2)}) async-start(), calls=%async_computation.10 | async-start | bytes 1572864 | tf_op jit(solution)/shard_map/reduce_scatter | solution.py:125
  224.5 6.2 %copy-start.8 = (bf16[256,2048]{1,0:T(8,128)(2,1)S(1)}, bf16[256,2048]{1,0:T(8,128)(2,1)}, u32[]{:S(2)}) copy-start(bf16[256,2048]{1,0:T(8,128)(2,1)} %all-gather.9.cloned.1.call-done) | copy-start | bytes 3145732
  230.7 9.6 %copy-start.16 = (s32[32]{0:T(128)S(1)}, s32[32]{0:T(128)}, u32[]{:S(2)}) copy-start(s32[32]{0:T(128)} %param.18) | copy-start | bytes 388
  230.7 19.6 %copy-start.10 = (bf16[256,512]{1,0:T(8,128)(2,1)S(1)}, bf16[256,512]{1,0:T(8,128)(2,1)}, u32[]{:S(2)}) copy-start(bf16[256,512]{1,0:T(8,128)(2,1)} %copy-done.9) | copy-start | bytes 786436
  230.7 30.2 %copy-start.6 = (bf16[256,4,64]{2,0,1:T(8,128)(2,1)S(1)}, bf16[256,4,64]{2,0,1:T(8,128)(2,1)}, u32[]{:S(2)}) copy-start(bf16[256,4,64]{2,0,1:T(8,128)(2,1)} %copy-done.5) | copy-start | bytes 393220
  240.3 32.0 %copy-start.3 = (bf16[256,1024]{1,0:T(8,128)(2,1)S(1)}, bf16[256,1024]{1,0:T(8,128)(2,1)}, u32[]{:S(2)}) copy-start(bf16[256,1024]{1,0:T(8,128)(2,1)} %add_convert_fusion.1) | copy-start | bytes 1572868
  243.3 11.0 %all-to-all-start = ((s32[16,16,1]{1,2,0:T(1,128)}), s32[16,16,1]{1,2,0:T(1,128)S(1)}, u32[]{:S(2)}, u32[]{:S(2)}) async-start(s32[16,16,1]{1,2,0:T(1,128)} %all_to_all.30), calls=%async_computation | async-start | bytes 16384 | tf_op jit(solution)/shard_map/all_to_all | solution.py:140
  254.3 10.7 %all-to-all-start.2 = ((s32[16,16,1]{1,2,0:T(1,128)}), s32[16,16,1]{1,2,0:T(1,128)S(1)}, u32[]{:S(2)}, u32[]{:S(2)}) async-start(s32[16,16,1]{1,2,0:T(1,128)} %all_to_all.35), calls=%async_computation.4 | async-start | bytes 16384 | tf_op jit(solution)/shard_map/all_to_all | solution.py:40
  265.0 18.6 %all-to-all-start.3 = ((bf16[16,16,1024]{2,1,0:T(8,128)(2,1)}), bf16[16,16,1024]{2,1,0:T(8,128)(2,1)}, u32[]{:S(2)}, u32[]{:S(2)}) async-start(bf16[16,16,1024]{2,1,0:T(8,128)(2,1)} %all_to_all.38), calls=%async_computation.5 | async-start | bytes 1048576 | tf_op jit(solution)/shard_map/all_to_all | solution.py:39
  272.3 31.3 %copy-start.1 = (bf16[2048,512]{1,0:T(8,128)(2,1)S(1)}, bf16[2048,512]{1,0:T(8,128)(2,1)}, u32[]{:S(2)}) copy-start(bf16[2048,512]{1,0:T(8,128)(2,1)} %param.21) | copy-start | bytes 6291460
  283.7 17.5 %all-to-all-start.1 = ((bf16[16,16,1024]{2,1,0:T(8,128)(2,1)}), bf16[16,16,1024]{2,1,0:T(8,128)(2,1)S(1)}, u32[]{:S(2)}, u32[]{:S(2)}) async-start(bf16[16,16,1024]{2,1,0:T(8,128)(2,1)} %bitcast.16), calls=%async_computation.3 | async-start | bytes 1048576 | tf_op jit(solution)/shard_map/all_to_all | solution.py:139
Sparse Core Ops, SparseCore 0:
  17.0 76.1 all-gather.6
  96.5 83.8 all-gather.4
  200.8 9.6 reduce-scatter.2
  212.7 10.1 all-gather.8
  240.5 9.6 reduce-scatter.4
where the time goes:
time: 314 us; the launch traced here: 310 us
  waiting for transfers between devices  131 us (42%)
  matrix products  60.8 us (19%)
  other arithmetic  31.1 us (10%)
  blocking collectives  28.6 us (9%)
  starting transfers between devices  27.1 us (9%)
  local copies, waits for them, and re-layouts  16.9 us (5%)
  between operations  14.2 us (5%)
    all_gather x1, waiting for transfers between devices, body(): piece_values = lax.all_gather(values, 'seq', axis=0, tiled=True)  56.3 us
    all_gather x1, waiting for transfers between devices, body(): piece_keys = lax.all_gather(knorm, 'seq', axis=0, tiled=True)  34.7 us
    all_gather x1, blocking collectives, body(): piece_order = lax.all_gather(token_order, 'seq', axis=0, tiled=True)  28.6 us
    dot_general x1, matrix products, body(): jnp.einsum('qkge,nke->qkgn', qnorm, piece_keys, preferred_element_type=jn...  16 us
    dot_general x1, matrix products, body(): jnp.einsum('qkgn,nke->qkge', weights.astype(jnp.bfloat16), piece_values,...  15.8 us
    reduce_sum x1, other arithmetic, body(): total = jnp.sum(weights, axis=-1)  14.9 us
    all_gather x1, waiting for transfers between devices, body(): mid_full = lax.all_gather(mid, 'tp', axis=1, tiled=True)  10.1 us
    dot_general x1, matrix products, body(): jnp.dot(act, down_weight, preferred_element_type=jnp.float32)  9.61 us
  transfers between devices with their start and end apart: 9, of which 8 were waited for; matrix products, arithmetic and copies ran while one was open for 18% of the time, Pallas kernels for 0%

commit v1 on v0

--- a/solution.py
+++ b/solution.py
@@ -29,8 +29,8 @@
 
 
 def request_start(order, lengths):
-    ends = jnp.cumsum(lengths)
-    begins = ends - lengths
+    index = jnp.arange(lengths.shape[0])
+    begins = jnp.sum(jnp.where(index[None, :] < index[:, None], lengths[None, :], 0), axis=1)
     return jnp.max(jnp.where(begins[None, :] <= order[:, None], begins[None, :], 0), axis=1)
 
 

time: 314 us -> 314 us (level)
  no operation moved by 1% of the time
where the time goes in v1:
time: 314 us; the launch traced here: 310 us
  waiting for transfers between devices  131 us (42%)
  matrix products  60.8 us (19%)
  other arithmetic  31 us (10%)
  blocking collectives  28.6 us (9%)
  starting transfers between devices  27.1 us (9%)
  local copies, waits for them, and re-layouts  16.9 us (5%)
  between operations  14.2 us (5%)
    all_gather x1, waiting for transfers between devices, body(): piece_values = lax.all_gather(values, 'seq', axis=0, tiled=True)  56.3 us
    all_gather x1, waiting for transfers between devices, body(): piece_keys = lax.all_gather(knorm, 'seq', axis=0, tiled=True)  34.7 us
    all_gather x1, blocking collectives, body(): piece_order = lax.all_gather(token_order, 'seq', axis=0, tiled=True)  28.6 us
    dot_general x1, matrix products, body(): jnp.einsum('qkge,nke->qkgn', qnorm, piece_keys, preferred_element_type=jn...  16 us
    dot_general x1, matrix products, body(): jnp.einsum('qkgn,nke->qkge', weights.astype(jnp.bfloat16), piece_values,...  15.8 us
    reduce_sum x1, other arithmetic, body(): total = jnp.sum(weights, axis=-1)  14.9 us
    all_gather x1, waiting for transfers between devices, body(): mid_full = lax.all_gather(mid, 'tp', axis=1, tiled=True)  10.1 us
    dot_general x1, matrix products, body(): jnp.dot(act, down_weight, preferred_element_type=jnp.float32)  9.6 us
  transfers between devices with their start and end apart: 9, of which 8 were waited for; matrix products, arithmetic and copies ran while one was open for 18% of the time, Pallas kernels for 0%

profile of v1, /device:TPU:14, one launch (start us, length us, event | category | flops | bytes accessed | tf_op | source)
XLA Modules:
  0.0 310.1 jit_solution(15350765585621969683)
XLA Ops:
  7.3 1.6 multiply_reduce_fusion
  9.1 2.9 fusion.47
  16.9 2.4 convolution_convert_fusion.2
  20.2 3.5 %convolution_bitcast_fusion = f32[32,8,8,128]{3,1,2,0:T(8,128)S(1)} fusion(bf16[2048,1024]{1,0:T(8,128)(2,1)} %param.20, f32[2048]{0:T(1024)S(1)} %copy-done.13, f32[256]{0:T(256)S(1)} %add_rsqrt_fusion.3, bf16[256,2048]{1,0:T(8,128)(2,1)S(1)} %copy-done.4), kind=kOutput, calls=%fused_computation.27 | convolution fusion | flops 1075838976 | bytes 6300672 | tf_op jit(solution)/shard_map/dot_general | solution.py:78
  26.4 1.5 subtract_convert_fusion
  28.0 28.6 %all-gather = s32[16,1,256]{2,1,0:T(1,128)S(1)} all-gather(s32[1,1,256]{2,1,0:T(1,128)S(1)} %bitcast.76), channel_id=1, replica_groups=mesh['seq'=16,'tp'=2] {'seq'}, dimensions={0}, use_global_device_ids=true | all-gather | bytes 17408 | tf_op jit(solution)/shard_map/all_gather | solution.py:93
  56.6 1.9 compare_and_fusion
  58.5 34.7 %all-gather.7.cloned.1.call-done = bf16[4096,4,128]{2,0,1:T(8,128)(2,1)} async-done(((bf16[256,4,128]{2,0,1:T(8,128)(2,1)}), bf16[4096,4,128]{2,0,1:T(8,128)(2,1)}) %all-gather.7.cloned.1.call-update) | async-done | bytes 4194320 | tf_op jit(solution)/shard_map/all_gather | solution.py:91
  93.2 16.0 %fusion = (f32[256,4,2]{0,2,1:T(2,128)S(1)}, f32[4,4096,256,2]{2,1,3,0:T(8,128)}) fusion(pred[256,4096]{0,1:T(8,128)(4,1)S(1)} %compare_and_fusion, bf16[256,4,2,64]{3,0,2,1:T(8,128)(2,1)S(1)} %bitcast.83, bf16[256,4,2,64]{3,0,2,1:T(8,128)(2,1)S(1)} %bitcast.84, bf16[4096,4,128]{2,0,1:T(8,128)(2,1)} %all-gather.7.cloned.1.call-done), kind=kOutput, calls=%fused_computation.6 | convolution fusion | flops 2173696000 | bytes 39329792 | tf_op jit(solution)/shard_map/qkge,nke->qkgn/dot_general | solution.py:95
  109.2 14.9 %fusion.1 = f32[256,4,2]{0,2,1:T(2,128)S(1)} fusion(f32[4,4096,256,2]{2,1,3,0:T(8,128)} %get-tuple-element.9, f32[256,4,2]{0,2,1:T(2,128)S(1)} %broadcast_maximum_fusion, pred[256,4096]{0,1:T(8,128)(4,1)S(1)} %compare_and_fusion), kind=kLoop, calls=%fused_computation.7 | loop fusion | flops 41940992 | bytes 34619392 | tf_op jit(solution)/shard_map/reduce_sum | solution.py:102
  124.1 56.3 %all-gather.5.cloned.1.call-done = bf16[4096,4,128]{0,2,1:T(8,128)(2,1)} async-done(((bf16[256,4,128]{0,2,1:T(8,128)(2,1)}), bf16[4096,4,128]{0,2,1:T(8,128)(2,1)}) %all-gather.5.cloned.1.call-update) | async-done | bytes 4194320 | tf_op jit(solution)/shard_map/all_gather | solution.py:92
  180.4 15.8 %fusion.23 = bf16[256,4,2,128]{0,3,2,1:T(8,128)(2,1)S(1)} fusion(f32[4,4096,256,2]{2,1,3,0:T(8,128)} %get-tuple-element.9, f32[256,4,2]{0,2,1:T(2,128)S(1)} %broadcast_maximum_fusion, pred[256,4096]{0,1:T(8,128)(4,1)S(1)} %compare_and_fusion, bf16[4096,4,128]{0,2,1:T(8,128)(2,1)} %all-gather.5.cloned.1.call-done, f32[256,4,2]{0,2,1:T(2,128)S(1)} %fusion.1), kind=kOutput, calls=%fused_computation.29 | convolution fusion | flops 2189950976 | bytes 39337984 | tf_op jit(solution)/shard_map/qkgn,nke->qkge/dot_general | solution.py:103
  196.2 4.4 %convolution_convert_fusion.1 = bf16[256,2048]{1,0:T(8,128)(2,1)} fusion(bf16[256,1024]{0,1:T(8,128)(2,1)S(1)} %bitcast.89, bf16[1024,2048]{1,0:T(8,128)(2,1)} %param.25), kind=kOutput, calls=%fused_computation.20 | convolution fusion | flops 1074266112 | bytes 5767168 | tf_op jit(solution)/shard_map/dot_general | solution.py:111
  201.0 9.6 %reduce-scatter.3.cloned.1.call-done = bf16[256,1024]{1,0:T(8,128)(2,1)} async-done(((bf16[256,2048]{1,0:T(8,128)(2,1)}), bf16[256,1024]{1,0:T(8,128)(2,1)}) %reduce-scatter.3.cloned.1.call-update) | async-done | bytes 524304 | tf_op jit(solution)/shard_map/reduce_scatter | solution.py:116
  210.5 2.0 add_convert_fusion.1
  212.8 10.1 %all-gather.9.cloned.1.call-done = bf16[256,2048]{1,0:T(8,128)(2,1)} async-done(((bf16[256,1024]{1,0:T(8,128)(2,1)}), bf16[256,2048]{1,0:T(8,128)(2,1)}) %all-gather.9.cloned.1.call-update) | async-done | bytes 1048592 | tf_op jit(solution)/shard_map/all_gather | solution.py:120
  222.9 1.5 fusion.10
  224.4 6.2 %fusion.34 = f32[256,1536]{1,0:T(8,128)} fusion(bf16[2048,1536]{1,0:T(8,128)(2,1)} %param.27, bf16[256,2048]{1,0:T(8,128)(2,1)} %all-gather.9.cloned.1.call-done, f32[2048]{0:T(1024)S(1)} %copy-done.14, f32[256]{0:T(256)S(1)} %add_rsqrt_fusion.2), kind=kOutput, calls=%fused_computation.46 | convolution fusion | flops 1612709888 | bytes 8922112 | tf_op jit(solution)/shard_map/dot_general | solution.py:122
  230.6 9.6 %convolution_convert_fusion = bf16[256,2048]{1,0:T(8,128)(2,1)} fusion(bf16[1536,2048]{1,0:T(8,128)(2,1)} %param.29, bf16[2048,1536]{1,0:T(8,128)(2,1)} %param.28, f32[256,1536]{1,0:T(8,128)} %fusion.34, bf16[256,2048]{1,0:T(8,128)(2,1)S(1)} %copy-done.8, f32[2048]{0:T(1024)S(1)} %copy-done.14, f32[256]{0:T(256)S(1)} %add_rsqrt_fusion.2), kind=kOutput, calls=%fused_computation.19 | convolution fusion | flops 3226206208 | bytes 16262144 | tf_op jit(solution)/shard_map/dot_general | solution.py:126
  240.6 1.9 gather_fusion
  243.2 7.0 %all-to-all-start = ((s32[16,16,1]{1,2,0:T(1,128)}), s32[16,16,1]{1,2,0:T(1,128)S(1)}, u32[]{:S(2)}, u32[]{:S(2)}) async-start(s32[16,16,1]{1,2,0:T(1,128)} %all_to_all.30), calls=%async_computation | async-start | bytes 16384 | tf_op jit(solution)/shard_map/all_to_all | solution.py:140
  251.0 3.3 %all-to-all-done = s32[16,16,1]{1,2,0:T(1,128)S(1)} async-done(((s32[16,16,1]{1,2,0:T(1,128)}), s32[16,16,1]{1,2,0:T(1,128)S(1)}, u32[]{:S(2)}, u32[]{:S(2)}) %all-to-all-start) | async-done | bytes 1056 | tf_op jit(solution)/shard_map/all_to_all | solution.py:140
  254.3 6.5 %all-to-all-start.2 = ((s32[16,16,1]{1,2,0:T(1,128)}), s32[16,16,1]{1,2,0:T(1,128)S(1)}, u32[]{:S(2)}, u32[]{:S(2)}) async-start(s32[16,16,1]{1,2,0:T(1,128)} %all_to_all.35), calls=%async_computation.4 | async-start | bytes 16384 | tf_op jit(solution)/shard_map/all_to_all | solution.py:40
  262.7 2.3 all-to-all-done.2
  265.0 7.2 %all-to-all-start.3 = ((bf16[16,16,1024]{2,1,0:T(8,128)(2,1)}), bf16[16,16,1024]{2,1,0:T(8,128)(2,1)}, u32[]{:S(2)}, u32[]{:S(2)}) async-start(bf16[16,16,1024]{2,1,0:T(8,128)(2,1)} %all_to_all.38), calls=%async_computation.5 | async-start | bytes 1048576 | tf_op jit(solution)/shard_map/all_to_all | solution.py:39
  272.3 1.4 add_convert_fusion
  273.7 2.0 gather_fusion.1
  275.6 8.0 %all-to-all-done.3 = bf16[16,16,1024]{2,1,0:T(8,128)(2,1)} async-done(((bf16[16,16,1024]{2,1,0:T(8,128)(2,1)}), bf16[16,16,1024]{2,1,0:T(8,128)(2,1)}, u32[]{:S(2)}, u32[]{:S(2)}) %all-to-all-start.3) | async-done | bytes 524320 | tf_op jit(solution)/shard_map/all_to_all | solution.py:39
  283.6 5.9 %all-to-all-start.1 = ((bf16[16,16,1024]{2,1,0:T(8,128)(2,1)}), bf16[16,16,1024]{2,1,0:T(8,128)(2,1)S(1)}, u32[]{:S(2)}, u32[]{:S(2)}) async-start(bf16[16,16,1024]{2,1,0:T(8,128)(2,1)} %bitcast.14), calls=%async_computation.3 | async-start | bytes 1048576 | tf_op jit(solution)/shard_map/all_to_all | solution.py:139
  290.9 3.0 scatter_custom_fusion.1
  293.9 7.2 %all-to-all-done.1 = bf16[16,16,1024]{2,1,0:T(8,128)(2,1)S(1)} async-done(((bf16[16,16,1024]{2,1,0:T(8,128)(2,1)}), bf16[16,16,1024]{2,1,0:T(8,128)(2,1)S(1)}, u32[]{:S(2)}, u32[]{:S(2)}) %all-to-all-start.1) | async-done | bytes 524320 | tf_op jit(solution)/shard_map/all_to_all | solution.py:139
  301.1 2.4 scatter_custom_fusion
  (90 shorter events, 14.4 us)
Async XLA Ops:
  7.2 1.9 copy-start
  7.2 6.4 %copy-start.15 = (s32[4]{0:T(128)S(1)}, s32[4]{0:T(128)}, u32[]{:S(2)}) copy-start(s32[4]{0:T(128)} %param.17) | copy-start | bytes 52
  7.2 6.6 %copy-start.2 = (s32[256]{0:T(256)S(1)}, s32[256]{0:T(256)}, u32[]{:S(2)}) copy-start(s32[256]{0:T(256)} %param.16) | copy-start | bytes 3076
  7.2 6.7 %copy-start.11 = (f32[128]{0:T(128)S(1)}, f32[128]{0:T(128)}, u32[]{:S(2)}) copy-start(f32[128]{0:T(128)} %param.24) | copy-start | bytes 1540
  7.2 85.9 %all-gather.7.cloned.1.call-start = ((), (), s32[]{:S(2)}) async-start(), calls=%async_computation.7 | async-start | bytes 4456448 | tf_op jit(solution)/shard_map/all_gather | solution.py:91
  9.1 7.8 %copy-start.4 = (bf16[256,2048]{1,0:T(8,128)(2,1)S(1)}, bf16[256,2048]{1,0:T(8,128)(2,1)}, u32[]{:S(2)}) copy-start(bf16[256,2048]{1,0:T(8,128)(2,1)} %param.15) | copy-start | bytes 3145732
  12.0 4.9 %copy-start.13 = (f32[2048]{0:T(1024)S(1)}, f32[2048]{0:T(1024)}, u32[]{:S(2)}) copy-start(f32[2048]{0:T(1024)} %param.19) | copy-start | bytes 24580
  15.6 4.5 %copy-start.7 = (f32[256,64]{1,0:T(8,128)}, f32[256,64]{1,0:T(8,128)S(1)}, u32[]{:S(2)}) copy-start(f32[256,64]{1,0:T(8,128)S(1)} %get-tuple-element.7) | copy-start | bytes 196612
  15.9 4.3 %copy-start.5 = (bf16[256,4,64]{2,0,1:T(8,128)(2,1)}, bf16[256,4,64]{2,0,1:T(8,128)(2,1)S(1)}, u32[]{:S(2)}) copy-start(bf16[256,4,64]{2,0,1:T(8,128)(2,1)S(1)} %get-tuple-element.5) | copy-start | bytes 393220
  16.8 163.6 %all-gather.5.cloned.1.call-start = ((), (), s32[]{:S(2)}) async-start(), calls=%async_computation.6 | async-start | bytes 4456448 | tf_op jit(solution)/shard_map/all_gather | solution.py:92
  19.2 1.0 copy-start.9
  20.1 5.0 %copy-start.12 = (f32[128]{0:T(128)S(1)}, f32[128]{0:T(128)}, u32[]{:S(2)}) copy-start(f32[128]{0:T(128)} %param.23) | copy-start | bytes 1540
  20.1 190.4 %reduce-scatter.3.cloned.1.call-start = ((), (), s32[]{:S(2)}) async-start(), calls=%async_computation.8 | async-start | bytes 1572864 | tf_op jit(solution)/shard_map/reduce_scatter | solution.py:116
  200.6 23.8 %copy-start.14 = (f32[2048]{0:T(1024)S(1)}, f32[2048]{0:T(1024)}, u32[]{:S(2)}) copy-start(f32[2048]{0:T(1024)} %param.26) | copy-start | bytes 24580
  200.7 22.2 %all-gather.9.cloned.1.call-start = ((), (), s32[]{:S(2)}) async-start(), calls=%async_computation.9 | async-start | bytes 1572864 | tf_op jit(solution)/shard_map/all_gather | solution.py:120
  212.5 59.7 %reduce-scatter.5.cloned.1.call-start = ((), (), s32[]{:S(2)}) async-start(), calls=%async_computation.10 | async-start | bytes 1572864 | tf_op jit(solution)/shard_map/reduce_scatter | solution.py:125
  224.4 6.2 %copy-start.8 = (bf16[256,2048]{1,0:T(8,128)(2,1)S(1)}, bf16[256,2048]{1,0:T(8,128)(2,1)}, u32[]{:S(2)}) copy-start(bf16[256,2048]{1,0:T(8,128)(2,1)} %all-gather.9.cloned.1.call-done) | copy-start | bytes 3145732
  230.6 9.6 %copy-start.16 = (s32[32]{0:T(128)S(1)}, s32[32]{0:T(128)}, u32[]{:S(2)}) copy-start(s32[32]{0:T(128)} %param.18) | copy-start | bytes 388
  230.6 19.6 %copy-start.10 = (bf16[256,512]{1,0:T(8,128)(2,1)S(1)}, bf16[256,512]{1,0:T(8,128)(2,1)}, u32[]{:S(2)}) copy-start(bf16[256,512]{1,0:T(8,128)(2,1)} %copy-done.9) | copy-start | bytes 786436
  230.6 30.2 %copy-start.6 = (bf16[256,4,64]{2,0,1:T(8,128)(2,1)S(1)}, bf16[256,4,64]{2,0,1:T(8,128)(2,1)}, u32[]{:S(2)}) copy-start(bf16[256,4,64]{2,0,1:T(8,128)(2,1)} %copy-done.5) | copy-start | bytes 393220
  240.2 32.0 %copy-start.3 = (bf16[256,1024]{1,0:T(8,128)(2,1)S(1)}, bf16[256,1024]{1,0:T(8,128)(2,1)}, u32[]{:S(2)}) copy-start(bf16[256,1024]{1,0:T(8,128)(2,1)} %add_convert_fusion.1) | copy-start | bytes 1572868
  243.2 11.0 %all-to-all-start = ((s32[16,16,1]{1,2,0:T(1,128)}), s32[16,16,1]{1,2,0:T(1,128)S(1)}, u32[]{:S(2)}, u32[]{:S(2)}) async-start(s32[16,16,1]{1,2,0:T(1,128)} %all_to_all.30), calls=%async_computation | async-start | bytes 16384 | tf_op jit(solution)/shard_map/all_to_all | solution.py:140
  254.3 10.7 %all-to-all-start.2 = ((s32[16,16,1]{1,2,0:T(1,128)}), s32[16,16,1]{1,2,0:T(1,128)S(1)}, u32[]{:S(2)}, u32[]{:S(2)}) async-start(s32[16,16,1]{1,2,0:T(1,128)} %all_to_all.35), calls=%async_computation.4 | async-start | bytes 16384 | tf_op jit(solution)/shard_map/all_to_all | solution.py:40
  265.0 18.6 %all-to-all-start.3 = ((bf16[16,16,1024]{2,1,0:T(8,128)(2,1)}), bf16[16,16,1024]{2,1,0:T(8,128)(2,1)}, u32[]{:S(2)}, u32[]{:S(2)}) async-start(bf16[16,16,1024]{2,1,0:T(8,128)(2,1)} %all_to_all.38), calls=%async_computation.5 | async-start | bytes 1048576 | tf_op jit(solution)/shard_map/all_to_all | solution.py:39
  272.2 31.3 %copy-start.1 = (bf16[2048,512]{1,0:T(8,128)(2,1)S(1)}, bf16[2048,512]{1,0:T(8,128)(2,1)}, u32[]{:S(2)}) copy-start(bf16[2048,512]{1,0:T(8,128)(2,1)} %param.21) | copy-start | bytes 6291460
  283.6 17.5 %all-to-all-start.1 = ((bf16[16,16,1024]{2,1,0:T(8,128)(2,1)}), bf16[16,16,1024]{2,1,0:T(8,128)(2,1)S(1)}, u32[]{:S(2)}, u32[]{:S(2)}) async-start(bf16[16,16,1024]{2,1,0:T(8,128)(2,1)} %bitcast.14), calls=%async_computation.3 | async-start | bytes 1048576 | tf_op jit(solution)/shard_map/all_to_all | solution.py:139
Sparse Core Ops, SparseCore 0:
  16.9 76.1 all-gather.6
  96.4 83.8 all-gather.4
  200.8 9.6 reduce-scatter.2
  212.7 10.1 all-gather.8
  240.4 9.6 reduce-scatter.4

commit v2 on v1

--- a/solution.py
+++ b/solution.py
@@ -1,6 +1,8 @@
 import jax
 import jax.numpy as jnp
 from jax import lax
+from jax.experimental import pallas as pl
+from jax.experimental.pallas import tpu as pltpu
 from jax.sharding import PartitionSpec as P
 
 HD = 128
@@ -145,6 +147,378 @@
     return (hidden_out, kv_cache)
 
 
+BF = jnp.bfloat16
+F32 = jnp.float32
+VMEM_BYTES = 56 * 1024 * 1024
+
+
+def project_kernel(x_ref, sel_ref, gain_ref, cos_ref, sin_ref, qg_ref, kg_ref, qw_ref, kw_ref, vw_ref,
+                   xs_ref, q_ref, kv_ref, stacked_ref, normed):
+    @pl.when(pl.program_id(0) == 0)
+    def _():
+        xs = jnp.dot(sel_ref[...], x_ref[...], preferred_element_type=F32)
+        xs_ref[...] = xs.astype(BF)
+        normed[...] = (
+            xs * lax.rsqrt(jnp.mean(xs * xs, axis=-1, keepdims=True) + EPS) * gain_ref[...]
+        ).astype(BF)
+
+    cosine, sine = cos_ref[...], sin_ref[...]
+
+    def turned(u, gain):
+        u = u * lax.rsqrt(jnp.mean(u * u, axis=-1, keepdims=True) + EPS) * gain
+        return (u * cosine + pltpu.roll(u, HD // 2, 1) * sine).astype(BF)
+
+    base = normed[...]
+    q = jnp.dot(base, qw_ref[...], preferred_element_type=F32)
+    q_ref[0, :, :HD] = turned(q[:, :HD], qg_ref[...])
+    q_ref[0, :, HD:] = turned(q[:, HD:], qg_ref[...])
+    k = turned(jnp.dot(base, kw_ref[...], preferred_element_type=F32), kg_ref[...])
+    v = jnp.dot(base, vw_ref[...], preferred_element_type=F32).astype(BF)
+    kv = jnp.concatenate([k, v], axis=1)
+    kv_ref[0] = kv
+    stacked_ref[...] = lax.dot_general(
+        sel_ref[...], kv, (((0,), (0,)), ((), ())), preferred_element_type=F32
+    ).astype(BF)
+
+
+def project(x, sel, gain, cosine, sine, qg, kg, qw, kw, vw):
+    rows, width = x.shape
+    heads = kw.shape[1] // HD
+    whole = lambda shape: pl.BlockSpec(shape, lambda h: (0, 0))
+    column = lambda cols: pl.BlockSpec((width, cols), lambda h: (0, h))
+    head = pl.BlockSpec((1, rows, 2 * HD), lambda h: (h, 0, 0))
+    return pl.pallas_call(
+        project_kernel,
+        grid=(heads,),
+        in_specs=[whole((rows, width)), whole((rows, rows)), whole((1, width)), whole((rows, HD)),
+                  whole((rows, HD)), whole((1, HD)), whole((1, HD)), column(2 * HD), column(HD), column(HD)],
+        out_specs=[whole((rows, width)), head, head, pl.BlockSpec((rows, 2 * HD), lambda h: (0, h))],
+        out_shape=[jax.ShapeDtypeStruct((rows, width), BF),
+                   jax.ShapeDtypeStruct((heads, rows, 2 * HD), BF),
+                   jax.ShapeDtypeStruct((heads, rows, 2 * HD), BF),
+                   jax.ShapeDtypeStruct((rows, heads * 2 * HD), BF)],
+        scratch_shapes=[pltpu.VMEM((rows, width), BF)],
+        compiler_params=pltpu.CompilerParams(vmem_limit_bytes=VMEM_BYTES),
+    )(x, sel, gain, cosine, sine, qg, kg, qw, kw, vw)
+
+
+def greet(seq_count, sibling):
+    barrier = pltpu.get_barrier_semaphore()
+    me = lax.axis_index("seq")
+    for k in range(1, seq_count):
+        pl.semaphore_signal(barrier, inc=1, device_id={"seq": lax.rem(me + k, seq_count)})
+    if sibling:
+        pl.semaphore_signal(barrier, inc=1, device_id={"tp": 1 - lax.axis_index("tp")})
+    pl.semaphore_wait(barrier, seq_count - 1 + (1 if sibling else 0))
+
+
+def push(src, dst, send, recv, **where):
+    return pltpu.make_async_remote_copy(
+        src_ref=src, dst_ref=dst, send_sem=send, recv_sem=recv, device_id=where
+    )
+
+
+def exchange_kernel(n, kv_ref, q_ref, order_ref, cache_ref, kv_out, q_out, order_out, cache_out,
+                    local, s1, r1, s2, r2, sq, rq, so, ro, sc, rc):
+    me = lax.axis_index("seq")
+    z, p = me // 4, lax.rem(me, 4)
+    part = lambda seq: pl.ds(pl.multiple_of(seq * 16, 16), 16)
+    own = [
+        pltpu.make_async_copy(kv_ref.at[z], kv_out.at[:, part(me), :], local.at[0]),
+        pltpu.make_async_copy(q_ref.at[z], q_out.at[:, part(z), :], local.at[1]),
+        pltpu.make_async_copy(order_ref, order_out.at[me], local.at[2]),
+        pltpu.make_async_copy(cache_ref.at[me], cache_out.at[me], local.at[3]),
+    ]
+    for copy in own:
+        copy.start()
+    greet(n, False)
+    first, second, query, orders, caches = [], [], [], [], []
+    for d in (1, 2, 3):
+        there = lax.rem(z + d, 4)
+        copy = push(kv_ref.at[there], kv_out.at[:, part(me), :], s1.at[d - 1], r1.at[d - 1], seq=there * 4 + p)
+        copy.start()
+        first.append(copy)
+    for k in (1, 2, 3):
+        copy = push(kv_ref.at[z], kv_out.at[:, part(me), :], s2.at[0, k - 1], r2.at[0, k - 1],
+                    seq=z * 4 + lax.rem(p + k, 4))
+        copy.start()
+        second.append(copy)
+    for k in range(1, n):
+        copy = push(order_ref, order_out.at[me], so.at[k - 1], ro.at[k - 1], seq=lax.rem(me + k, n))
+        copy.start()
+        orders.append(copy)
+    for d in (1, 2, 3):
+        there = lax.rem(z + d, 4)
+        copy = push(q_ref.at[there], q_out.at[:, part(z), :], sq.at[d - 1], rq.at[d - 1], seq=there * 4 + p)
+        copy.start()
+        query.append(copy)
+    for d in (1, 3, 2):
+        first[d - 1].wait_recv()
+        rows = part(lax.rem(z + 4 - d, 4) * 4 + p)
+        for k in (1, 2, 3):
+            copy = push(kv_out.at[:, rows, :], kv_out.at[:, rows, :], s2.at[d, k - 1], r2.at[d, k - 1],
+                        seq=z * 4 + lax.rem(p + k, 4))
+            copy.start()
+            second.append(copy)
+    for k in range(1, n):
+        there = lax.rem(me + k, n)
+        copy = push(cache_ref.at[there], cache_out.at[me], sc.at[k - 1], rc.at[k - 1], seq=there)
+        copy.start()
+        caches.append(copy)
+    for copy in own:
+        copy.wait()
+    for copy in first:
+        copy.wait_send()
+    for copy in second + query + orders + caches:
+        copy.wait()
+
+
+def exchange(kv, q, orders, cache, n):
+    heads = kv.shape[0]
+    dma = pltpu.SemaphoreType.DMA
+    anywhere = pl.BlockSpec(memory_space=pl.ANY)
+    width = kv.shape[-1]
+    return pl.pallas_call(
+        lambda *refs: exchange_kernel(n, *refs),
+        in_specs=[anywhere] * 4,
+        out_specs=[anywhere] * 4,
+        out_shape=[jax.ShapeDtypeStruct((n, n * 16, width), BF),
+                   jax.ShapeDtypeStruct((n, 4 * 16, width), BF),
+                   jax.ShapeDtypeStruct((n,) + orders.shape, jnp.int32),
+                   jax.ShapeDtypeStruct(cache.shape, BF)],
+        scratch_shapes=[dma((4,)), dma((3,)), dma((3,)), dma((4, 3)), dma((4, 3)), dma((3,)), dma((3,)),
+                        dma((n - 1,)), dma((n - 1,)), dma((n - 1,)), dma((n - 1,))],
+        compiler_params=pltpu.CompilerParams(collective_id=0, has_side_effects=True),
+    )(kv, q, orders, cache)
+
+
+def attend_kernel(low_ref, q_ref, kv_ref, info_ref, key_ref, out_ref):
+    i = pl.program_id(0)
+    q = q_ref[...].reshape(128, 2 * HD)
+    both = jnp.concatenate([q[:, :HD], q[:, HD:]], axis=0)
+    token, begin = info_ref[:, 0:1], info_ref[:, 1:2]
+    scale = 1.0 / HD**0.5
+
+    key_all = key_ref[...]
+    which = lax.broadcasted_iota(jnp.int32, key_all.shape, 0)
+
+    def step(j, carry):
+        best, total, accum = carry
+        kv = kv_ref[pl.ds(2 * j, 2)].reshape(512, 2 * HD)
+        score = lax.dot_general(
+            both, kv[:, :HD], (((1,), (1,)), ((), ())), preferred_element_type=F32
+        ) * scale
+        keys = jnp.sum(jnp.where(which == j, key_all, 0), axis=0, keepdims=True)
+        mask = (keys >= begin) & (keys <= token)
+        score = jnp.where(jnp.concatenate([mask, mask], axis=0), score, -1e30)
+        new_best = jnp.maximum(best, jnp.max(score, axis=1, keepdims=True))
+        weights = jnp.exp(score - new_best)
+        shrink = jnp.exp(best - new_best)
+        total = total * shrink + jnp.sum(weights, axis=1, keepdims=True)
+        accum = accum * shrink + jnp.dot(weights.astype(BF), kv[:, HD:], preferred_element_type=F32)
+        return new_best, total, accum
+
+    start = (jnp.full((256, 1), -1e30, F32), jnp.zeros((256, 1), F32), jnp.zeros((256, HD), F32))
+    _, total, accum = lax.fori_loop(low_ref[i], i + 1, step, start)
+    attn = (accum / total).astype(BF)
+    out_ref[...] = jnp.concatenate([attn[:128], attn[128:]], axis=1).reshape(2, 64, 2 * HD)
+
+
+def attend(low, q, kv, info, keys):
+    tiles = q.shape[0] // 2
+    block = pl.BlockSpec((2, 64, 2 * HD), lambda i, low: (i, 0, 0))
+    return pl.pallas_call(
+        attend_kernel,
+        grid_spec=pltpu.PrefetchScalarGridSpec(
+            num_scalar_prefetch=1,
+            grid=(tiles,),
+            in_specs=[block, pl.BlockSpec(kv.shape, lambda i, low: (0, 0, 0)),
+                      pl.BlockSpec((128, 2), lambda i, low: (i, 0)),
+                      pl.BlockSpec(keys.shape, lambda i, low: (0, 0))],
+            out_specs=block,
+        ),
+        out_shape=jax.ShapeDtypeStruct(q.shape, BF),
+        compiler_params=pltpu.CompilerParams(vmem_limit_bytes=VMEM_BYTES),
+    )(low, q, kv, info, keys)
+
+
+def finish_kernel(n, attn_ref, xs_ref, gain_ref, place_ref, wo_hbm, wg_hbm, wu_hbm, wd_hbm, out_ref,
+                  wo, wg, wu, wd, attn, terms, sent, came, mid, normed, act, half_out, half_in, ready, arrived,
+                  wsem, local, sa, ra, st, rt, sf, rf, sx, rx):
+    me, t = lax.axis_index("seq"), lax.axis_index("tp")
+    z, p = me // 4, lax.rem(me, 4)
+    part = lambda seq: pl.ds(pl.multiple_of(seq * 16, 16), 16)
+    loads = [pltpu.make_async_copy(a, b, wsem.at[i])
+             for i, (a, b) in enumerate(((wo_hbm, wo), (wg_hbm, wg), (wu_hbm, wu), (wd_hbm, wd)))]
+    for load in loads:
+        load.start()
+    keep = pltpu.make_async_copy(attn_ref.at[:, part(z), :], attn.at[z], local.at[0])
+    keep.start()
+    greet(n, True)
+    moves = []
+    for d in (1, 2, 3):
+        there = lax.rem(z + d, 4)
+        copy = push(attn_ref.at[:, part(there), :], attn.at[z], sa.at[d - 1], ra.at[d - 1], seq=there * 4 + p)
+        copy.start()
+        moves.append(copy)
+    loads[0].wait()
+    keep.wait()
+    for copy in moves:
+        copy.wait()
+    rows, width = xs_ref.shape
+    part_width = width // 2
+    tile = 256
+    column = lambda j: pl.ds(pl.multiple_of(j * tile, tile), tile)
+
+    @pl.loop(0, width // tile)
+    def _(j):
+        result = jnp.zeros((rows, tile), F32)
+        for h in range(4):
+            result += jnp.dot(attn[h].reshape(rows, 2 * HD), wo[h * 256:(h + 1) * 256, column(j)],
+                              preferred_element_type=F32)
+        sent[:, column(j)] = result.astype(BF)
+
+    swap = push(sent, came, st.at[0], rt.at[0], tp=1 - t)
+    swap.start()
+    swap.wait()
+    full = xs_ref[...].astype(F32) + (sent[...].astype(F32) + came[...].astype(F32))
+    mid[...] = full.astype(BF)
+    full = mid[...].astype(F32)
+    normed[...] = (
+        full * lax.rsqrt(jnp.mean(full * full, axis=-1, keepdims=True) + EPS) * gain_ref[...]
+    ).astype(BF)
+    loads[1].wait()
+    loads[2].wait()
+
+    @pl.loop(0, act.shape[1] // tile)
+    def _(j):
+        gate = jnp.dot(normed[...], wg[:, column(j)], preferred_element_type=F32)
+        upper = jnp.dot(normed[...], wu[:, column(j)], preferred_element_type=F32)
+        act[:, column(j)] = (gate * jax.nn.sigmoid(gate) * upper).astype(BF)
+
+    loads[3].wait()
+    steps = part_width // tile
+
+    @pl.loop(0, steps)
+    def _(j):
+        half_out[:, column(j)] = jnp.dot(
+            act[...], wd[:, column((1 - t) * steps + j)], preferred_element_type=F32
+        ).astype(BF)
+
+    swap = push(half_out, half_in, sf.at[0], rf.at[0], tp=1 - t)
+    swap.start()
+
+    @pl.loop(0, steps)
+    def _(j):
+        terms[:, column(j)] = jnp.dot(act[...], wd[:, column(t * steps + j)], preferred_element_type=F32)
+
+    swap.wait()
+
+    @pl.loop(0, steps)
+    def _(j):
+        out = mid[:, column(t * steps + j)].astype(F32) + (
+            terms[:, column(j)] + half_in[:, column(j)].astype(F32)
+        )
+        ready[:, :, column(j)] = out.astype(BF).reshape(n, rows // n, tile)
+
+    keep = pltpu.make_async_copy(ready.at[me], arrived.at[me], local.at[1])
+    keep.start()
+    moves = []
+    for k in range(1, n):
+        there = lax.rem(me + k, n)
+        copy = push(ready.at[there], arrived.at[me], sx.at[k - 1], rx.at[k - 1], seq=there)
+        copy.start()
+        moves.append(copy)
+    keep.wait()
+    for copy in moves:
+        copy.wait()
+
+    @pl.loop(0, steps)
+    def _(j):
+        out_ref[:, column(j)] = jnp.dot(
+            place_ref[...], arrived[:, :, column(j)].reshape(rows, tile), preferred_element_type=F32
+        ).astype(BF)
+
+
+def finish(attn, xs, gain, place, wo, wg, wu, wd, n):
+    rows, width = xs.shape
+    half, hidden = width // 2, wg.shape[1]
+    dma = pltpu.SemaphoreType.DMA
+    vmem = pl.BlockSpec(memory_space=pltpu.VMEM)
+    anywhere = pl.BlockSpec(memory_space=pl.ANY)
+    room = lambda *shape: pltpu.VMEM(shape, BF)
+    return pl.pallas_call(
+        lambda *refs: finish_kernel(n, *refs),
+        in_specs=[anywhere, vmem, vmem, vmem] + [anywhere] * 4,
+        out_specs=vmem,
+        out_shape=jax.ShapeDtypeStruct((rows, half), BF),
+        scratch_shapes=[room(*wo.shape), room(*wg.shape), room(*wu.shape), room(*wd.shape),
+                        room(4, n, rows // n, 2 * HD), pltpu.VMEM((rows, half), F32),
+                        room(rows, width), room(rows, width), room(rows, width), room(rows, width),
+                        room(rows, hidden), room(rows, half), room(rows, half),
+                        room(n, rows // n, half), room(n, rows // n, half),
+                        dma((4,)), dma((2,)), dma((3,)), dma((3,)), dma((1,)), dma((1,)), dma((1,)), dma((1,)),
+                        dma((n - 1,)), dma((n - 1,))],
+        compiler_params=pltpu.CompilerParams(
+            collective_id=1, has_side_effects=True, vmem_limit_bytes=VMEM_BYTES
+        ),
+    )(attn, xs, gain, place, wo, wg, wu, wd)
+
+
+def fast_body(
+    hidden_in, token_order, span_lengths, placement, norm_in, q_weight, k_weight, v_weight, q_gain, k_gain,
+    o_weight, norm_mid, gate_weight, up_weight, down_weight,
+):
+    rows, width = hidden_in.shape
+    n = lax.axis_size("seq")
+    me = lax.axis_index("seq")
+    share = BLK // n
+    slot_rows = (placement[:, None] * share + jnp.arange(share, dtype=jnp.int32)[None, :]).reshape(rows)
+    chosen = slot_rows[:, None] == jnp.arange(rows, dtype=jnp.int32)[None, :]
+    order = jnp.sum(jnp.where(chosen, token_order[None, :], 0), axis=1)
+    pos = order - request_start(order, span_lengths)
+    half = HD // 2
+    freq = THETA ** (-jnp.arange(half, dtype=F32) * 2.0 / HD)
+    angle = pos.astype(F32)[:, None] * freq[None, :]
+    cosine, sine = jnp.cos(angle), jnp.sin(angle)
+    cosine = jnp.concatenate([cosine, cosine], axis=1)
+    sine = jnp.concatenate([-sine, sine], axis=1)
+    xs, q, kv, stacked = project(
+        hidden_in, chosen.astype(BF), norm_in[None, :], cosine, sine, q_gain[None, :], k_gain[None, :],
+        q_weight, k_weight, v_weight,
+    )
+    group = rows // n
+    split = lambda a: a.reshape(a.shape[0], n, group, a.shape[2])
+    orders = jnp.concatenate(
+        [order[None, :], token_order[None, :], jnp.zeros((6, rows), jnp.int32)], axis=0
+    )
+    kv_all, q_all, orders_all, cache_all = exchange(
+        split(kv), split(q), orders, stacked.reshape(n, group, stacked.shape[1]), n
+    )
+    by_pair = orders_all[:, 0, :].reshape(n, n, group)
+    keys = by_pair.transpose(1, 0, 2).reshape(n // 2, 2 * n * group)
+    mine = lax.dynamic_index_in_dim(by_pair.reshape(4, 4, n, group), lax.rem(me, 4), 1, keepdims=False)
+    token = mine.transpose(1, 0, 2).reshape(n * 4 * group)
+    info = jnp.stack([token, request_start(token, span_lengths)], axis=1)
+    low = request_start(jnp.arange(n // 2, dtype=jnp.int32) * (2 * rows), span_lengths) // (2 * rows)
+    attn = attend(low, q_all, kv_all, info, keys)
+    row_ids = jnp.arange(rows, dtype=jnp.int32)
+    landed = lax.dynamic_index_in_dim(by_pair, me, 1, keepdims=False).reshape(rows) - me * rows
+    place = (row_ids[:, None] == landed[None, :]).astype(BF)
+    hidden_out = finish(
+        attn, xs, norm_mid[None, :], place, o_weight, gate_weight, up_weight, down_weight, n
+    )
+    anchor = lax.dynamic_index_in_dim(
+        orders_all[:, 1, :].reshape(n, n, group), me, 1, keepdims=False
+    ).reshape(rows)
+    target = row_ids % group // share * BLK + anchor % BLK
+    to_cache = (row_ids[:, None] == target[None, :]).astype(BF)
+    kv_cache = jnp.dot(
+        to_cache, cache_all.reshape(rows, stacked.shape[1]), preferred_element_type=F32
+    ).astype(BF).reshape(rows // BLK, BLK, stacked.shape[1])
+    return (hidden_out, kv_cache)
+
+
 def solution(mesh):
     in_specs = (
         P("seq", None),
@@ -164,4 +538,5 @@
         P("tp", None),
     )
     out_specs = (P("seq", "tp"), P("seq", None, "tp"))
-    return jax.shard_map(body, mesh=mesh, in_specs=in_specs, out_specs=out_specs, check_vma=False)
+    chosen = fast_body if mesh.shape["seq"] == 16 and mesh.shape["tp"] == 2 else body
+    return jax.shard_map(chosen, mesh=mesh, in_specs=in_specs, out_specs=out_specs, check_vma=False)

time: 314 us -> 128 us (0.41)
  waiting for transfers between devices: 131 us -> 0 us
  Pallas kernels: 0 us -> 110 us
  matrix products: 60.8 us -> 2.14 us
  blocking collectives: 28.6 us -> 0 us
  starting transfers between devices: 27.1 us -> 0 us
  other arithmetic: 31 us -> 7.42 us
  between operations: 14.2 us -> 0.75 us
  local copies, waits for them, and re-layouts: 16.9 us -> 5.51 us
    pallas_call x0 -> x4, Pallas kernels: none -> 110 us  [the longest x1 44.5 us: finish(): pl.pallas_call(lambda *refs: finish_kernel(n, *refs), in_specs=[anywhere,...]
    all_gather x3 -> x0, waiting for transfers between devices: 101 us -> none  [the longest x1 56.3 us: body(): piece_values = lax.all_gather(values, 'seq', axis=0, tiled=True)]
    dot_general x8 -> x1, matrix products: 60.8 us -> 2.14 us  [fast_body(): jnp.dot(to_cache, cache_all.reshape(rows, stacked.shape[1]), preferred_el...]
    all_gather x1 -> x0, blocking collectives: 28.6 us -> none  [body(): piece_order = lax.all_gather(token_order, 'seq', axis=0, tiled=True)]
    all_to_all x4 -> x0, starting transfers between devices: 26.7 us -> none  [the longest x1 7.25 us: relay_cache(): lax.all_to_all(stacked, 'seq', split_axis=0, concat_axis=0, tiled=True)]
    all_to_all x4 -> x0, waiting for transfers between devices: 20.7 us -> none  [the longest x1 8 us: relay_cache(): lax.all_to_all(stacked, 'seq', split_axis=0, concat_axis=0, tiled=True)]
    reduce_sum x5 -> x1, other arithmetic: 18.7 us -> 0.86 us  [fast_body(): order = jnp.sum(jnp.where(chosen, token_order[None, :], 0), axis=1)]
    reduce_scatter x2 -> x0, waiting for transfers between devices: 9.59 us -> none  [the longest x1 9.57 us: body(): lax.psum_scatter(terms.astype(jnp.bfloat16), 'tp', scatter_dimension=1, t...]
  transfers between devices with their start and end apart: 9 -> 0, of which waited for: 8 -> 0; matrix products, arithmetic and copies ran while one was open for 18% -> 0% of each run, Pallas kernels for 0% -> 0%
where the time goes in v2:
time: 128 us; the launch traced here: 126 us
  Pallas kernels  110 us (86%)
  other arithmetic  7.42 us (6%)
  local copies, waits for them, and re-layouts  5.51 us (4%)
  matrix products  2.14 us (2%)
    pallas_call x1, Pallas kernels, finish(): pl.pallas_call(lambda *refs: finish_kernel(n, *refs), in_specs=[anywhere,...  44.5 us
    pallas_call x1, Pallas kernels, exchange(): pl.pallas_call(lambda *refs: exchange_kernel(n, *refs), in_specs=[anywher...  43.8 us
    pallas_call x1, Pallas kernels, attend(): pl.pallas_call(attend_kernel, grid_spec=pltpu.PrefetchScalarGridSpec(num_...  12.8 us
    pallas_call x1, Pallas kernels, project(): pl.pallas_call(project_kernel, grid=(heads,), in_specs=[whole((rows, widt...  8.99 us

profile of v2, /device:TPU:14, one launch (start us, length us, event | category | flops | bytes accessed | tf_op | source)
XLA Modules:
  0.0 125.9 jit_solution(8263026563515561439)
XLA Ops:
  0.6 0.7 broadcast_multiply_fusion
  1.3 0.1 iota_add_fusion
  1.4 0.1 add.63
  1.5 0.9 select_reduce_fusion
  2.3 0.8 select_reduce_fusion.4
  3.1 0.1 select_reduce_fusion.2
  3.2 0.5 fusion.3
  3.7 0.8 pad_maximum_fusion.1.sin_ref
  4.5 0.8 pad_maximum_fusion.cos_ref
  5.3 0.7 fusion.sel_ref
  6.0 9.0 %shard_map.158 = (bf16[256,2048]{1,0:T(8,128)(2,1)}, bf16[4,256,256]{2,1,0:T(8,128)(2,1)}, bf16[4,256,256]{2,1,0:T(8,128)(2,1)}, bf16[256,1024]{1,0:T(8,128)(2,1)}) custom-call(bf16[256,2048]{1,0:T(8,128)(2,1)} %x_ref.1, bf16[256,256]{1,0:T(8,128)(2,1)} %fusion.sel_ref, f32[1,2048]{1,0:T(1,128)} %bitcast.32, f32[256,128]{1,0:T(8,128)} %pad_maximum_fusion.cos_ref, ...), custom_call_target="tpu_custom_call" | custom-call | tf_op jit(solution)/shard_map/pallas_call | solution.py:190
  15.0 0.1 pad.4.clone
  15.1 0.7 add_add_fusion.refs_2_
  15.8 43.8 %shard_map.159 = (bf16[16,256,256]{2,1,0:T(8,128)(2,1)}, bf16[16,64,256]{2,1,0:T(8,128)(2,1)}, s32[16,8,256]{2,1,0:T(8,128)}, bf16[16,16,1024]{2,1,0:T(8,128)(2,1)}) custom-call(bf16[4,16,16,256]{3,2,1,0:T(8,128)(2,1)} %bitcast.22, bf16[4,16,16,256]{3,2,1,0:T(8,128)(2,1)} %bitcast.21, s32[8,256]{1,0:T(8,128)} %add_add_fusion.refs_2_, ...), custom_call_target="tpu_custom_call" | custom-call | tf_op jit(solution)/shard_map/pallas_call | solution.py:281
  59.6 1.1 slice_reduce_fusion
  60.6 0.1 reshape_squeeze.6
  60.7 0.1 reshape_squeeze.7
  60.9 0.1 reshape.123
  61.0 2.1 %convolution_convert_fusion = bf16[256,1024]{1,0:T(8,128)(2,1)} fusion(bf16[256,1024]{1,0:T(8,128)(2,1)} %bitcast.25, s32[256]{0:T(256)S(1)} %fusion.4), kind=kOutput, calls=%fused_computation | convolution fusion | flops 134545408 | bytes 1049600 | tf_op jit(solution)/shard_map/dot_general | solution.py:516
  63.2 0.1 sub.34
  63.2 0.7 fusion.1.refs_3_
  63.9 0.1 reshape_reshape_squeeze.3
  64.1 0.1 le.48
  64.1 0.1 select_reduce_fusion.1
  64.2 0.1 stack_reshape.3
  64.4 1.0 copy.28.info_ref
  65.4 0.7 reshape.122.key_ref
  66.1 0.1 select_reduce_fusion.3
  66.2 0.5 and_select_fusion.3.low_ref
  66.8 12.8 %shard_map.160.refs_0_ = bf16[16,64,256]{2,1,0:T(8,128)(2,1)} custom-call(s32[8]{0:T(128)} %and_select_fusion.3.low_ref, bf16[16,64,256]{2,1,0:T(8,128)(2,1)} %get-tuple-element.13.q_ref, bf16[16,256,256]{2,1,0:T(8,128)(2,1)} %get-tuple-element.14.kv_ref, s32[1024,2]{1,0:T(8,128)} %copy.28.info_ref, s32[8,512]{1,0:T(8,128)} %reshape.122.key_ref), custom_call_target="tpu_custom_call" | custom-call | tf_op jit(solution)/shard_map/pallas_call | solution.py:330
  79.5 44.5 %shard_map.161 = bf16[256,1024]{1,0:T(8,128)(2,1)} custom-call(bf16[16,64,256]{2,1,0:T(8,128)(2,1)} %shard_map.160.refs_0_, bf16[256,2048]{1,0:T(8,128)(2,1)} %get-tuple-element.16.refs_1_, f32[1,2048]{1,0:T(1,128)} %bitcast.31, bf16[256,256]{1,0:T(8,128)(2,1)} %fusion.1.refs_3_, bf16[1024,2048]{1,0:T(8,128)(2,1)} %refs_4_.1, bf16[2048,1536]{1,0:T(8,128)(2,1)} %refs_5_.1, ...), custom_call_target="tpu_custom_call" | custom-call | tf_op jit(solution)/shard_map/pallas_call | solution.py:450
  124.0 1.9 %copy.34 = bf16[256,1024]{1,0:T(8,128)(2,1)} copy(bf16[256,1024]{1,0:T(8,128)(2,1)} %shard_map.161) | data formatting | bytes 1048576
  (12 shorter events, 0.2 us)
Async XLA Ops:
  6.0 9.1 %copy-start = (s32[256]{0:T(256)S(1)}, s32[256]{0:T(256)}, u32[]{:S(2)}) copy-start(s32[256]{0:T(256)} %param.16) | copy-start | bytes 3076

commit v3 on v2

--- a/solution.py
+++ b/solution.py
@@ -218,8 +218,8 @@
     )
 
 
-def exchange_kernel(n, kv_ref, q_ref, order_ref, cache_ref, kv_out, q_out, order_out, cache_out,
-                    local, s1, r1, s2, r2, sq, rq, so, ro, sc, rc):
+def exchange_kernel(n, kv_ref, q_ref, order_ref, kv_out, q_out, order_out,
+                    local, s1, r1, s2, r2, sq, rq, so, ro):
     me = lax.axis_index("seq")
     z, p = me // 4, lax.rem(me, 4)
     part = lambda seq: pl.ds(pl.multiple_of(seq * 16, 16), 16)
@@ -227,12 +227,11 @@
         pltpu.make_async_copy(kv_ref.at[z], kv_out.at[:, part(me), :], local.at[0]),
         pltpu.make_async_copy(q_ref.at[z], q_out.at[:, part(z), :], local.at[1]),
         pltpu.make_async_copy(order_ref, order_out.at[me], local.at[2]),
-        pltpu.make_async_copy(cache_ref.at[me], cache_out.at[me], local.at[3]),
     ]
     for copy in own:
         copy.start()
     greet(n, False)
-    first, second, query, orders, caches = [], [], [], [], []
+    first, second, query, orders = [], [], [], []
     for d in (1, 2, 3):
         there = lax.rem(z + d, 4)
         copy = push(kv_ref.at[there], kv_out.at[:, part(me), :], s1.at[d - 1], r1.at[d - 1], seq=there * 4 + p)
@@ -260,36 +259,30 @@
                         seq=z * 4 + lax.rem(p + k, 4))
             copy.start()
             second.append(copy)
-    for k in range(1, n):
-        there = lax.rem(me + k, n)
-        copy = push(cache_ref.at[there], cache_out.at[me], sc.at[k - 1], rc.at[k - 1], seq=there)
-        copy.start()
-        caches.append(copy)
     for copy in own:
         copy.wait()
     for copy in first:
         copy.wait_send()
-    for copy in second + query + orders + caches:
+    for copy in second + query + orders:
         copy.wait()
 
 
-def exchange(kv, q, orders, cache, n):
+def exchange(kv, q, orders, n):
     heads = kv.shape[0]
     dma = pltpu.SemaphoreType.DMA
     anywhere = pl.BlockSpec(memory_space=pl.ANY)
     width = kv.shape[-1]
     return pl.pallas_call(
         lambda *refs: exchange_kernel(n, *refs),
-        in_specs=[anywhere] * 4,
-        out_specs=[anywhere] * 4,
+        in_specs=[anywhere] * 3,
+        out_specs=[anywhere] * 3,
         out_shape=[jax.ShapeDtypeStruct((n, n * 16, width), BF),
                    jax.ShapeDtypeStruct((n, 4 * 16, width), BF),
-                   jax.ShapeDtypeStruct((n,) + orders.shape, jnp.int32),
-                   jax.ShapeDtypeStruct(cache.shape, BF)],
-        scratch_shapes=[dma((4,)), dma((3,)), dma((3,)), dma((4, 3)), dma((4, 3)), dma((3,)), dma((3,)),
-                        dma((n - 1,)), dma((n - 1,)), dma((n - 1,)), dma((n - 1,))],
+                   jax.ShapeDtypeStruct((n,) + orders.shape, jnp.int32)],
+        scratch_shapes=[dma((3,)), dma((3,)), dma((3,)), dma((4, 3)), dma((4, 3)), dma((3,)), dma((3,)),
+                        dma((n - 1,)), dma((n - 1,))],
         compiler_params=pltpu.CompilerParams(collective_id=0, has_side_effects=True),
-    )(kv, q, orders, cache)
+    )(kv, q, orders)
 
 
 def attend_kernel(low_ref, q_ref, kv_ref, info_ref, key_ref, out_ref):
@@ -342,9 +335,9 @@
     )(low, q, kv, info, keys)
 
 
-def finish_kernel(n, attn_ref, xs_ref, gain_ref, place_ref, wo_hbm, wg_hbm, wu_hbm, wd_hbm, out_ref,
-                  wo, wg, wu, wd, attn, terms, sent, came, mid, normed, act, half_out, half_in, ready, arrived,
-                  wsem, local, sa, ra, st, rt, sf, rf, sx, rx):
+def finish_kernel(n, attn_ref, xs_ref, gain_ref, cache_ref, wo_hbm, wg_hbm, wu_hbm, wd_hbm, arrived, cache_out,
+                  wo, wg, wu, wd, attn, sent, came, mid, normed, act, half_out, half_in, ready,
+                  wsem, local, sa, ra, st, rt, sf, rf, sx, rx, sc, rc):
     me, t = lax.axis_index("seq"), lax.axis_index("tp")
     z, p = me // 4, lax.rem(me, 4)
     part = lambda seq: pl.ds(pl.multiple_of(seq * 16, 16), 16)
@@ -354,6 +347,8 @@
         load.start()
     keep = pltpu.make_async_copy(attn_ref.at[:, part(z), :], attn.at[z], local.at[0])
     keep.start()
+    late = [pltpu.make_async_copy(cache_ref.at[me], cache_out.at[me], local.at[1])]
+    late[0].start()
     greet(n, True)
     moves = []
     for d in (1, 2, 3):
@@ -361,32 +356,44 @@
         copy = push(attn_ref.at[:, part(there), :], attn.at[z], sa.at[d - 1], ra.at[d - 1], seq=there * 4 + p)
         copy.start()
         moves.append(copy)
+    for k in range(1, n):
+        there = lax.rem(me + k, n)
+        copy = push(cache_ref.at[there], cache_out.at[me], sc.at[k - 1], rc.at[k - 1], seq=there)
+        copy.start()
+        late.append(copy)
     loads[0].wait()
     keep.wait()
     for copy in moves:
         copy.wait()
     rows, width = xs_ref.shape
-    part_width = width // 2
     tile = 256
     column = lambda j: pl.ds(pl.multiple_of(j * tile, tile), tile)
-
-    @pl.loop(0, width // tile)
-    def _(j):
+    swaps = []
+    for j in range(width // tile):
         result = jnp.zeros((rows, tile), F32)
         for h in range(4):
-            result += jnp.dot(attn[h].reshape(rows, 2 * HD), wo[h * 256:(h + 1) * 256, column(j)],
+            result += jnp.dot(attn[h].reshape(rows, 2 * HD), wo[h * 256:(h + 1) * 256, j * tile:(j + 1) * tile],
                               preferred_element_type=F32)
-        sent[:, column(j)] = result.astype(BF)
-
-    swap = push(sent, came, st.at[0], rt.at[0], tp=1 - t)
-    swap.start()
-    swap.wait()
-    full = xs_ref[...].astype(F32) + (sent[...].astype(F32) + came[...].astype(F32))
-    mid[...] = full.astype(BF)
-    full = mid[...].astype(F32)
-    normed[...] = (
-        full * lax.rsqrt(jnp.mean(full * full, axis=-1, keepdims=True) + EPS) * gain_ref[...]
-    ).astype(BF)
+        sent[:, j * tile:(j + 1) * tile] = result.astype(BF)
+        if j % 2:
+            c = j // 2
+            both = pl.ds(c * 2 * tile, 2 * tile)
+            swap = push(sent.at[:, both], came.at[:, both], st.at[c], rt.at[c], tp=1 - t)
+            swap.start()
+            swaps.append(swap)
+    square = jnp.zeros((rows, 1), F32)
+    for c, swap in enumerate(swaps):
+        swap.wait()
+        cols = slice(c * 2 * tile, (c + 1) * 2 * tile)
+        piece = xs_ref[:, cols].astype(F32) + (sent[:, cols].astype(F32) + came[:, cols].astype(F32))
+        piece = piece.astype(BF)
+        mid[:, cols] = piece
+        piece = piece.astype(F32)
+        square += jnp.sum(piece * piece, axis=-1, keepdims=True)
+    factor = lax.rsqrt(square / width + EPS)
+    for c in range(len(swaps)):
+        cols = slice(c * 2 * tile, (c + 1) * 2 * tile)
+        normed[:, cols] = (mid[:, cols].astype(F32) * factor * gain_ref[:, cols]).astype(BF)
     loads[1].wait()
     loads[2].wait()
 
@@ -397,50 +404,39 @@
         act[:, column(j)] = (gate * jax.nn.sigmoid(gate) * upper).astype(BF)
 
     loads[3].wait()
-    steps = part_width // tile
-
-    @pl.loop(0, steps)
-    def _(j):
-        half_out[:, column(j)] = jnp.dot(
+    steps = width // 2 // tile
+    swaps = []
+    for j in range(steps):
+        cols = pl.ds(j * tile, tile)
+        half_out[:, cols] = jnp.dot(
             act[...], wd[:, column((1 - t) * steps + j)], preferred_element_type=F32
         ).astype(BF)
-
-    swap = push(half_out, half_in, sf.at[0], rf.at[0], tp=1 - t)
-    swap.start()
-
-    @pl.loop(0, steps)
-    def _(j):
-        terms[:, column(j)] = jnp.dot(act[...], wd[:, column(t * steps + j)], preferred_element_type=F32)
-
-    swap.wait()
-
-    @pl.loop(0, steps)
-    def _(j):
-        out = mid[:, column(t * steps + j)].astype(F32) + (
-            terms[:, column(j)] + half_in[:, column(j)].astype(F32)
-        )
-        ready[:, :, column(j)] = out.astype(BF).reshape(n, rows // n, tile)
-
-    keep = pltpu.make_async_copy(ready.at[me], arrived.at[me], local.at[1])
-    keep.start()
-    moves = []
-    for k in range(1, n):
-        there = lax.rem(me + k, n)
-        copy = push(ready.at[there], arrived.at[me], sx.at[k - 1], rx.at[k - 1], seq=there)
-        copy.start()
-        moves.append(copy)
-    keep.wait()
-    for copy in moves:
+        swap = push(half_out.at[:, cols], half_in.at[:, cols], sf.at[j], rf.at[j], tp=1 - t)
+        swap.start()
+        swaps.append(swap)
+    for j in range(steps):
+        cols = pl.ds(j * tile, tile)
+        term = jnp.dot(act[...], wd[:, column(t * steps + j)], preferred_element_type=F32)
+        swaps[j].wait()
+        out = mid[:, column(t * steps + j)].astype(F32) + (term + half_in[:, cols].astype(F32))
+        ready[:, :, cols] = out.astype(BF).reshape(n, rows // n, tile)
+        if j % 2:
+            c = j // 2
+            both = pl.ds(c * 2 * tile, 2 * tile)
+            copy = pltpu.make_async_copy(ready.at[me, :, both], arrived.at[me, :, both], local.at[2 + c])
+            copy.start()
+            late.append(copy)
+            for k in range(1, n):
+                there = lax.rem(me + k, n)
+                copy = push(ready.at[there, :, both], arrived.at[me, :, both], sx.at[c, k - 1], rx.at[c, k - 1],
+                            seq=there)
+                copy.start()
+                late.append(copy)
+    for copy in late:
         copy.wait()
 
-    @pl.loop(0, steps)
-    def _(j):
-        out_ref[:, column(j)] = jnp.dot(
-            place_ref[...], arrived[:, :, column(j)].reshape(rows, tile), preferred_element_type=F32
-        ).astype(BF)
-
-
-def finish(attn, xs, gain, place, wo, wg, wu, wd, n):
+
+def finish(attn, xs, gain, cache, wo, wg, wu, wd, n):
     rows, width = xs.shape
     half, hidden = width // 2, wg.shape[1]
     dma = pltpu.SemaphoreType.DMA
@@ -449,20 +445,42 @@
     room = lambda *shape: pltpu.VMEM(shape, BF)
     return pl.pallas_call(
         lambda *refs: finish_kernel(n, *refs),
-        in_specs=[anywhere, vmem, vmem, vmem] + [anywhere] * 4,
-        out_specs=vmem,
-        out_shape=jax.ShapeDtypeStruct((rows, half), BF),
+        in_specs=[anywhere, vmem, vmem] + [anywhere] * 5,
+        out_specs=[anywhere] * 2,
+        out_shape=[jax.ShapeDtypeStruct((n, rows // n, half), BF), jax.ShapeDtypeStruct(cache.shape, BF)],
         scratch_shapes=[room(*wo.shape), room(*wg.shape), room(*wu.shape), room(*wd.shape),
-                        room(4, n, rows // n, 2 * HD), pltpu.VMEM((rows, half), F32),
+                        room(4, n, rows // n, 2 * HD),
                         room(rows, width), room(rows, width), room(rows, width), room(rows, width),
                         room(rows, hidden), room(rows, half), room(rows, half),
-                        room(n, rows // n, half), room(n, rows // n, half),
-                        dma((4,)), dma((2,)), dma((3,)), dma((3,)), dma((1,)), dma((1,)), dma((1,)), dma((1,)),
-                        dma((n - 1,)), dma((n - 1,))],
+                        room(n, rows // n, half),
+                        dma((4,)), dma((4,)), dma((3,)), dma((3,)), dma((4,)), dma((4,)), dma((4,)), dma((4,)),
+                        dma((2, n - 1)), dma((2, n - 1)), dma((n - 1,)), dma((n - 1,))],
         compiler_params=pltpu.CompilerParams(
             collective_id=1, has_side_effects=True, vmem_limit_bytes=VMEM_BYTES
         ),
-    )(attn, xs, gain, place, wo, wg, wu, wd)
+    )(attn, xs, gain, cache, wo, wg, wu, wd)
+
+
+def unsort_kernel(landed_ref, target_ref, out_ref, cache_ref, hidden_ref, kv_ref):
+    rows = out_ref.shape[0]
+    row = lax.broadcasted_iota(jnp.int32, (rows, rows), 0)
+    for index, source, result in ((landed_ref, out_ref, hidden_ref), (target_ref, cache_ref, kv_ref)):
+        chosen = jnp.where(row == index[...], 1.0, 0.0).astype(BF)
+        result[...] = jnp.dot(chosen, source[...], preferred_element_type=F32).astype(BF)
+
+
+def unsort(landed, target, out, cache):
+    rows, width = out.shape
+    tile = 512
+    index = pl.BlockSpec((1, rows), lambda j: (0, 0))
+    block = pl.BlockSpec((rows, tile), lambda j: (0, j))
+    return pl.pallas_call(
+        unsort_kernel,
+        grid=(width // tile,),
+        in_specs=[index, index, block, block],
+        out_specs=[block, block],
+        out_shape=[jax.ShapeDtypeStruct(out.shape, BF), jax.ShapeDtypeStruct(cache.shape, BF)],
+    )(landed, target, out, cache)
 
 
 def fast_body(
@@ -479,10 +497,10 @@
     pos = order - request_start(order, span_lengths)
     half = HD // 2
     freq = THETA ** (-jnp.arange(half, dtype=F32) * 2.0 / HD)
-    angle = pos.astype(F32)[:, None] * freq[None, :]
-    cosine, sine = jnp.cos(angle), jnp.sin(angle)
-    cosine = jnp.concatenate([cosine, cosine], axis=1)
-    sine = jnp.concatenate([-sine, sine], axis=1)
+    lane = jnp.arange(HD)
+    angle = pos.astype(F32)[:, None] * jnp.tile(freq, 2)[None, :]
+    cosine = jnp.cos(angle)
+    sine = jnp.sin(angle) * jnp.where(lane < half, -1.0, 1.0)[None, :]
     xs, q, kv, stacked = project(
         hidden_in, chosen.astype(BF), norm_in[None, :], cosine, sine, q_gain[None, :], k_gain[None, :],
         q_weight, k_weight, v_weight,
@@ -492,9 +510,7 @@
     orders = jnp.concatenate(
         [order[None, :], token_order[None, :], jnp.zeros((6, rows), jnp.int32)], axis=0
     )
-    kv_all, q_all, orders_all, cache_all = exchange(
-        split(kv), split(q), orders, stacked.reshape(n, group, stacked.shape[1]), n
-    )
+    kv_all, q_all, orders_all = exchange(split(kv), split(q), orders, n)
     by_pair = orders_all[:, 0, :].reshape(n, n, group)
     keys = by_pair.transpose(1, 0, 2).reshape(n // 2, 2 * n * group)
     mine = lax.dynamic_index_in_dim(by_pair.reshape(4, 4, n, group), lax.rem(me, 4), 1, keepdims=False)
@@ -504,18 +520,19 @@
     attn = attend(low, q_all, kv_all, info, keys)
     row_ids = jnp.arange(rows, dtype=jnp.int32)
     landed = lax.dynamic_index_in_dim(by_pair, me, 1, keepdims=False).reshape(rows) - me * rows
-    place = (row_ids[:, None] == landed[None, :]).astype(BF)
-    hidden_out = finish(
-        attn, xs, norm_mid[None, :], place, o_weight, gate_weight, up_weight, down_weight, n
-    )
     anchor = lax.dynamic_index_in_dim(
         orders_all[:, 1, :].reshape(n, n, group), me, 1, keepdims=False
     ).reshape(rows)
     target = row_ids % group // share * BLK + anchor % BLK
-    to_cache = (row_ids[:, None] == target[None, :]).astype(BF)
-    kv_cache = jnp.dot(
-        to_cache, cache_all.reshape(rows, stacked.shape[1]), preferred_element_type=F32
-    ).astype(BF).reshape(rows // BLK, BLK, stacked.shape[1])
+    cache_width = stacked.shape[1]
+    arrived, cache_all = finish(
+        attn, xs, norm_mid[None, :], stacked.reshape(n, group, cache_width),
+        o_weight, gate_weight, up_weight, down_weight, n
+    )
+    hidden_out, kv_cache = unsort(
+        landed[None, :], target[None, :], arrived.reshape(rows, width // 2), cache_all.reshape(rows, cache_width)
+    )
+    kv_cache = kv_cache.reshape(rows // BLK, BLK, cache_width)
     return (hidden_out, kv_cache)
 
 

time: 128 us -> 123 us (0.961)
  matrix products: 2.14 us -> 0 us
    pallas_call x1, Pallas kernels: 43.8 us -> 37.7 us  [exchange(): pl.pallas_call(lambda *refs: exchange_kernel(n, *refs), in_specs=[anywher...]
    pallas_call x1, Pallas kernels: 44.5 us -> 47.7 us  [finish(): pl.pallas_call(lambda *refs: finish_kernel(n, *refs), in_specs=[anywhere,...]
    pallas_call x0 -> x1, Pallas kernels: none -> 2.41 us  [unsort(): pl.pallas_call(unsort_kernel, grid=(width // tile,), in_specs=[index, ind...]
    dot_general x1 -> x0, matrix products: 2.14 us -> none  [fast_body(): jnp.dot(to_cache, cache_all.reshape(rows, stacked.shape[1]), preferred_el...]
    unnamed x3 -> x2, local copies, waits for them, and re-layouts: 1.87 us -> 0.01 us
    concatenate x2 -> x0, other arithmetic: 1.52 us -> none  [the longest x1 0.77 us: fast_body(): sine = jnp.concatenate([-sine, sine], axis=1)]
where the time goes in v3:
time: 123 us; the launch traced here: 122 us
  Pallas kernels  111 us (90%)
  other arithmetic  6.46 us (5%)
  local copies, waits for them, and re-layouts  4.29 us (3%)
    pallas_call x1, Pallas kernels, finish(): pl.pallas_call(lambda *refs: finish_kernel(n, *refs), in_specs=[anywhere,...  47.7 us
    pallas_call x1, Pallas kernels, exchange(): pl.pallas_call(lambda *refs: exchange_kernel(n, *refs), in_specs=[anywher...  37.7 us
    pallas_call x1, Pallas kernels, attend(): pl.pallas_call(attend_kernel, grid_spec=pltpu.PrefetchScalarGridSpec(num_...  13.8 us
    pallas_call x1, Pallas kernels, project(): pl.pallas_call(project_kernel, grid=(heads,), in_specs=[whole((rows, widt...  8.99 us

profile of v3, /device:TPU:14, one launch (start us, length us, event | category | flops | bytes accessed | tf_op | source)
XLA Modules:
  0.0 122.1 jit_solution(18426726686677352648)
XLA Ops:
  0.6 0.7 broadcast_multiply_fusion
  1.3 0.1 iota_add_fusion
  1.4 0.1 add.75
  1.5 0.7 fusion.sel_ref
  2.2 0.1 mul.59
  2.3 0.9 select_reduce_fusion
  3.2 0.8 select_reduce_fusion.4
  3.9 0.1 select_reduce_fusion.2
  4.0 1.3 %fusion.1 = (f32[256,128]{1,0:T(8,128)}, f32[256,128]{1,0:T(8,128)}) fusion(f32[128]{0:T(128)S(1)} %compare_select_fusion.5, f32[128]{0:T(128)S(1)} %mul.59, f32[256]{0:T(256)S(1)} %subtract_convert_fusion), kind=kLoop, calls=%fused_computation.5 | loop fusion | flops 65536 | bytes 264192 | tf_op jit(solution)/shard_map/mul | solution.py:503
  5.3 0.0 copy-start
  5.3 9.0 %shard_map.158 = (bf16[256,2048]{1,0:T(8,128)(2,1)}, bf16[4,256,256]{2,1,0:T(8,128)(2,1)}, bf16[4,256,256]{2,1,0:T(8,128)(2,1)}, bf16[256,1024]{1,0:T(8,128)(2,1)}) custom-call(bf16[256,2048]{1,0:T(8,128)(2,1)} %x_ref.1, bf16[256,256]{1,0:T(8,128)(2,1)} %fusion.sel_ref, f32[1,2048]{1,0:T(1,128)} %bitcast.38, f32[256,128]{1,0:T(8,128)} %get-tuple-element.29.cos_ref, ...), custom_call_target="tpu_custom_call" | custom-call | tf_op jit(solution)/shard_map/pallas_call | solution.py:190
  14.3 0.1 pad.4.clone
  14.4 0.0 copy-done
  14.4 0.7 add_add_fusion.refs_2_
  15.0 37.7 %shard_map.159 = (bf16[16,256,256]{2,1,0:T(8,128)(2,1)}, bf16[16,64,256]{2,1,0:T(8,128)(2,1)}, s32[16,8,256]{2,1,0:T(8,128)}) custom-call(bf16[4,16,16,256]{3,2,1,0:T(8,128)(2,1)} %bitcast.29, bf16[4,16,16,256]{3,2,1,0:T(8,128)(2,1)} %bitcast.28, s32[8,256]{1,0:T(8,128)} %add_add_fusion.refs_2_), custom_call_target="tpu_custom_call" | custom-call | tf_op jit(solution)/shard_map/pallas_call | solution.py:275
  52.8 1.1 slice_reduce_fusion
  53.8 0.1 reshape_squeeze.6
  54.0 0.6 sub.36.landed_ref
  54.6 0.1 reshape_squeeze.7
  54.7 0.1 reshape.213
  54.8 0.6 fusion.2.target_ref
  55.4 0.1 select_reduce_fusion.3
  55.5 0.5 and_select_fusion.3.low_ref
  56.0 0.1 reshape_reshape_squeeze.3
  56.2 0.1 le.48
  56.3 0.1 select_reduce_fusion.1
  56.4 0.1 stack_reshape.3
  56.5 1.0 copy.36.info_ref
  57.5 0.7 reshape.214.key_ref
  58.2 13.8 %shard_map.160.refs_0_ = bf16[16,64,256]{2,1,0:T(8,128)(2,1)} custom-call(s32[8]{0:T(128)} %and_select_fusion.3.low_ref, bf16[16,64,256]{2,1,0:T(8,128)(2,1)} %get-tuple-element.16.q_ref, bf16[16,256,256]{2,1,0:T(8,128)(2,1)} %get-tuple-element.17.kv_ref, s32[1024,2]{1,0:T(8,128)} %copy.36.info_ref, s32[8,512]{1,0:T(8,128)} %reshape.214.key_ref), custom_call_target="tpu_custom_call" | custom-call | tf_op jit(solution)/shard_map/pallas_call | solution.py:323
  72.0 47.7 %shard_map.161 = (bf16[16,16,1024]{2,1,0:T(8,128)(2,1)}, bf16[16,16,1024]{2,1,0:T(8,128)(2,1)}) custom-call(bf16[16,64,256]{2,1,0:T(8,128)(2,1)} %shard_map.160.refs_0_, bf16[256,2048]{1,0:T(8,128)(2,1)} %get-tuple-element.18.refs_1_, f32[1,2048]{1,0:T(1,128)} %bitcast.37, bf16[16,16,1024]{2,1,0:T(8,128)(2,1)} %bitcast.27, bf16[1024,2048]{1,0:T(8,128)(2,1)} %refs_4_.1, ...), custom_call_target="tpu_custom_call" | custom-call | tf_op jit(solution)/shard_map/pallas_call | solution.py:446
  119.7 2.4 %shard_map.162 = (bf16[256,1024]{1,0:T(8,128)(2,1)}, bf16[256,1024]{1,0:T(8,128)(2,1)}) custom-call(s32[1,256]{1,0:T(1,128)} %sub.36.landed_ref, s32[1,256]{1,0:T(1,128)} %fusion.2.target_ref, bf16[256,1024]{1,0:T(8,128)(2,1)} %bitcast.30, bf16[256,1024]{1,0:T(8,128)(2,1)} %bitcast.31), custom_call_target="tpu_custom_call" | custom-call | tf_op jit(solution)/shard_map/pallas_call | solution.py:477
  (12 shorter events, 0.1 us)
Async XLA Ops:
  5.3 9.1 %copy-start = (s32[256]{0:T(256)S(1)}, s32[256]{0:T(256)}, u32[]{:S(2)}) copy-start(s32[256]{0:T(256)} %param.16) | copy-start | bytes 3076

commit v4 on v3

--- a/solution.py
+++ b/solution.py
@@ -356,15 +356,15 @@
         copy = push(attn_ref.at[:, part(there), :], attn.at[z], sa.at[d - 1], ra.at[d - 1], seq=there * 4 + p)
         copy.start()
         moves.append(copy)
-    for k in range(1, n):
-        there = lax.rem(me + k, n)
-        copy = push(cache_ref.at[there], cache_out.at[me], sc.at[k - 1], rc.at[k - 1], seq=there)
-        copy.start()
-        late.append(copy)
     loads[0].wait()
     keep.wait()
     for copy in moves:
         copy.wait()
+    for k in range(1, n):
+        there = lax.rem(me + k, n)
+        copy = push(cache_ref.at[there], cache_out.at[me], sc.at[k - 1], rc.at[k - 1], seq=there)
+        copy.start()
+        late.append(copy)
     rows, width = xs_ref.shape
     tile = 256
     column = lambda j: pl.ds(pl.multiple_of(j * tile, tile), tile)

time: 123 us -> 118 us (0.959)
  Pallas kernels: 111 us -> 105 us
    pallas_call x1, Pallas kernels: 47.7 us -> 41.2 us  [finish(): pl.pallas_call(lambda *refs: finish_kernel(n, *refs), in_specs=[anywhere,...]
where the time goes in v4:
time: 118 us; the launch traced here: 116 us
  Pallas kernels  105 us (89%)
  other arithmetic  6.46 us (5%)
  local copies, waits for them, and re-layouts  4.29 us (4%)
    pallas_call x1, Pallas kernels, finish(): pl.pallas_call(lambda *refs: finish_kernel(n, *refs), in_specs=[anywhere,...  41.2 us
    pallas_call x1, Pallas kernels, exchange(): pl.pallas_call(lambda *refs: exchange_kernel(n, *refs), in_specs=[anywher...  37.7 us
    pallas_call x1, Pallas kernels, attend(): pl.pallas_call(attend_kernel, grid_spec=pltpu.PrefetchScalarGridSpec(num_...  14.4 us
    pallas_call x1, Pallas kernels, project(): pl.pallas_call(project_kernel, grid=(heads,), in_specs=[whole((rows, widt...  8.99 us
    pallas_call x1, Pallas kernels, unsort(): pl.pallas_call(unsort_kernel, grid=(width // tile,), in_specs=[index, ind...  2.41 us

profile of v4, /device:TPU:14, one launch (start us, length us, event | category | flops | bytes accessed | tf_op | source)
XLA Modules:
  0.0 116.2 jit_solution(15718163181087517770)
XLA Ops:
  0.6 0.7 broadcast_multiply_fusion
  1.3 0.1 iota_add_fusion
  1.4 0.1 add.75
  1.5 0.7 fusion.sel_ref
  2.2 0.1 mul.59
  2.3 0.9 select_reduce_fusion
  3.2 0.8 select_reduce_fusion.4
  3.9 0.1 select_reduce_fusion.2
  4.0 1.3 %fusion.1 = (f32[256,128]{1,0:T(8,128)}, f32[256,128]{1,0:T(8,128)}) fusion(f32[128]{0:T(128)S(1)} %compare_select_fusion.5, f32[128]{0:T(128)S(1)} %mul.59, f32[256]{0:T(256)S(1)} %subtract_convert_fusion), kind=kLoop, calls=%fused_computation.5 | loop fusion | flops 65536 | bytes 264192 | tf_op jit(solution)/shard_map/mul | solution.py:503
  5.3 0.0 copy-start
  5.3 9.0 %shard_map.158 = (bf16[256,2048]{1,0:T(8,128)(2,1)}, bf16[4,256,256]{2,1,0:T(8,128)(2,1)}, bf16[4,256,256]{2,1,0:T(8,128)(2,1)}, bf16[256,1024]{1,0:T(8,128)(2,1)}) custom-call(bf16[256,2048]{1,0:T(8,128)(2,1)} %x_ref.1, bf16[256,256]{1,0:T(8,128)(2,1)} %fusion.sel_ref, f32[1,2048]{1,0:T(1,128)} %bitcast.38, f32[256,128]{1,0:T(8,128)} %get-tuple-element.29.cos_ref, ...), custom_call_target="tpu_custom_call" | custom-call | tf_op jit(solution)/shard_map/pallas_call | solution.py:190
  14.3 0.1 pad.4.clone
  14.4 0.0 copy-done
  14.4 0.7 add_add_fusion.refs_2_
  15.0 37.7 %shard_map.159 = (bf16[16,256,256]{2,1,0:T(8,128)(2,1)}, bf16[16,64,256]{2,1,0:T(8,128)(2,1)}, s32[16,8,256]{2,1,0:T(8,128)}) custom-call(bf16[4,16,16,256]{3,2,1,0:T(8,128)(2,1)} %bitcast.29, bf16[4,16,16,256]{3,2,1,0:T(8,128)(2,1)} %bitcast.28, s32[8,256]{1,0:T(8,128)} %add_add_fusion.refs_2_), custom_call_target="tpu_custom_call" | custom-call | tf_op jit(solution)/shard_map/pallas_call | solution.py:275
  52.8 1.1 slice_reduce_fusion
  53.8 0.1 reshape_squeeze.6
  54.0 0.6 sub.36.landed_ref
  54.6 0.1 reshape_squeeze.7
  54.7 0.1 reshape.213
  54.8 0.6 fusion.2.target_ref
  55.4 0.1 select_reduce_fusion.3
  55.5 0.5 and_select_fusion.3.low_ref
  56.0 0.1 reshape_reshape_squeeze.3
  56.2 0.1 le.48
  56.3 0.1 select_reduce_fusion.1
  56.4 0.1 stack_reshape.3
  56.5 1.0 copy.36.info_ref
  57.5 0.7 reshape.214.key_ref
  58.2 14.4 %shard_map.160.refs_0_ = bf16[16,64,256]{2,1,0:T(8,128)(2,1)} custom-call(s32[8]{0:T(128)} %and_select_fusion.3.low_ref, bf16[16,64,256]{2,1,0:T(8,128)(2,1)} %get-tuple-element.16.q_ref, bf16[16,256,256]{2,1,0:T(8,128)(2,1)} %get-tuple-element.17.kv_ref, s32[1024,2]{1,0:T(8,128)} %copy.36.info_ref, s32[8,512]{1,0:T(8,128)} %reshape.214.key_ref), custom_call_target="tpu_custom_call" | custom-call | tf_op jit(solution)/shard_map/pallas_call | solution.py:323
  72.6 41.2 %shard_map.161 = (bf16[16,16,1024]{2,1,0:T(8,128)(2,1)}, bf16[16,16,1024]{2,1,0:T(8,128)(2,1)}) custom-call(bf16[16,64,256]{2,1,0:T(8,128)(2,1)} %shard_map.160.refs_0_, bf16[256,2048]{1,0:T(8,128)(2,1)} %get-tuple-element.18.refs_1_, f32[1,2048]{1,0:T(1,128)} %bitcast.37, bf16[16,16,1024]{2,1,0:T(8,128)(2,1)} %bitcast.27, bf16[1024,2048]{1,0:T(8,128)(2,1)} %refs_4_.1, ...), custom_call_target="tpu_custom_call" | custom-call | tf_op jit(solution)/shard_map/pallas_call | solution.py:446
  113.8 2.4 %shard_map.162 = (bf16[256,1024]{1,0:T(8,128)(2,1)}, bf16[256,1024]{1,0:T(8,128)(2,1)}) custom-call(s32[1,256]{1,0:T(1,128)} %sub.36.landed_ref, s32[1,256]{1,0:T(1,128)} %fusion.2.target_ref, bf16[256,1024]{1,0:T(8,128)(2,1)} %bitcast.30, bf16[256,1024]{1,0:T(8,128)(2,1)} %bitcast.31), custom_call_target="tpu_custom_call" | custom-call | tf_op jit(solution)/shard_map/pallas_call | solution.py:477
  (12 shorter events, 0.1 us)
Async XLA Ops:
  5.3 9.1 %copy-start = (s32[256]{0:T(256)S(1)}, s32[256]{0:T(256)}, u32[]{:S(2)}) copy-start(s32[256]{0:T(256)} %param.16) | copy-start | bytes 3076
